TPU v7x, 256 devices: a whole 4x4x8 slice. The times are simulated.
256 devices in a mesh: row: 8 (over x_lo, y), col: 32 (over z, x_hi, core).
Axes of the slice: x: 4 (x_hi: 2, x_lo: 2; x = x_hi * 2 + x_lo), y: 4, z: 8, core: 2. Of those that a mesh axis runs over, the one named last changes fastest.
Arguments:
- noise: float32 [4096, 4096], P('row', 'col'), may hold values from -20 to 20
- data: float32 [16384, 4096], P('col', 'row'), may hold values from -20 to 20
Outputs:
- noise_target: float32 [4096, 4096], P(('row', 'col'))
- data_target: float32 [16384, 4096], P('col', 'row')
All inputs are finite; a program needn't handle non-finite values.
Results may differ from a plain program's by a relative error of at most 0.012.
The roundings to bfloat16 on the way count: a program that leaves them out, or rounds other values in their place, can miss the bound.
Values may be sent and summed in bfloat16 or wider, within the bound.
A program may use at most 64 MiB of HBM per device.

v0:
```python
import math

import jax
import jax.numpy as jnp
from jax import lax
from jax.sharding import PartitionSpec as P

ITERS = 3


entropy_weight = 0.25


def row_softmin(scores):
    local_max = jnp.max(scores, axis=1)
    largest = lax.pmax(local_max, "col")
    summed = lax.psum(jnp.sum(jnp.exp(scores - largest[:, None]), axis=1), "col")
    return largest + jnp.log(summed)


def col_softmin(scores):
    local_max = jnp.max(scores, axis=0)
    largest = lax.pmax(local_max, "row")
    summed = lax.psum(jnp.sum(jnp.exp(scores - largest[None, :]), axis=0), "row")
    return largest + jnp.log(summed)


def local(noise, data):
    noise_half = noise.astype(jnp.bfloat16)
    data_half = data.astype(jnp.bfloat16)
    data_block = lax.all_gather(data_half, "row", axis=1, tiled=True)
    noise_rows = noise.shape[0]
    data_rows = data.shape[0]
    features = data_block.shape[1]
    log_rows = math.log(noise_rows * lax.axis_size("row"))
    log_cols = math.log(data_rows * lax.axis_size("col"))
    data_square = jnp.sum(jnp.square(data_block.astype(jnp.float32)), axis=1)
    noise_block = None
    noise_block = lax.all_gather(noise_half, "col", axis=1, tiled=True)
    noise_square = jnp.sum(jnp.square(noise_block.astype(jnp.float32)), axis=1)
    products = jnp.einsum("nk,mk->nm", noise_block, data_block, preferred_element_type=jnp.float32)
    distance = (noise_square[:, None] + data_square[None, :] - 2.0 * products) / features
    pot_data = jnp.zeros((data_rows,), jnp.float32)
    pot_noise = jnp.zeros((noise_rows,), jnp.float32)
    for iteration in range(ITERS):
        pot_noise = -entropy_weight * (
            row_softmin((pot_data[None, :] - distance) / entropy_weight) + log_rows
        )
        pot_data = -entropy_weight * (
            col_softmin((pot_noise[:, None] - distance) / entropy_weight) + log_cols
        )
    coupling = jnp.exp(
        (pot_noise[:, None] + pot_data[None, :] - distance) / entropy_weight + log_rows + log_cols
    ).astype(jnp.bfloat16)
    row_mass = lax.psum(jnp.sum(coupling.astype(jnp.float32), axis=1), "col")
    col_mass = lax.psum(jnp.sum(coupling.astype(jnp.float32), axis=0), "row")
    share = noise_rows // lax.axis_size("col")
    noise_sum = lax.psum_scatter(
        jnp.dot(coupling, data_block, preferred_element_type=jnp.float32),
        "col",
        scatter_dimension=0,
        tiled=True,
    )
    own_mass = lax.dynamic_slice_in_dim(row_mass, lax.axis_index("col") * share, share, 0)
    noise_target = noise_sum / own_mass[:, None]
    data_partial = jnp.einsum(
        "nm,nk->mk", coupling, noise_block, preferred_element_type=jnp.float32
    )
    data_sum = lax.psum_scatter(data_partial, "row", scatter_dimension=1, tiled=True)
    data_target = data_sum / col_mass[:, None]
    return (noise_target, data_target)


def solution(mesh):
    return jax.shard_map(
        local,
        mesh=mesh,
        in_specs=(P("row", "col"), P("col", "row")),
        out_specs=(P(("row", "col"), None), P("col", "row")),
        check_vma=False,
    )
```

profile of v0, /device:TPU:32, one launch (start us, length us, event | category | flops | bytes accessed | tf_op | source)
XLA Modules:
  0.0 926.4 jit_solution(5074490259258106610)
XLA Ops:
  7.2 0.0 all-gather.5.cloned.1.call-start
  7.2 2.1 convert_element_type.21
  9.3 0.0 all-gather.5.cloned.1.call-update
  9.3 0.0 all-gather.3.cloned.1.call-start
  9.4 1.6 convert_element_type.19
  11.0 0.0 all-gather.3.cloned.1.call-update
  11.0 0.0 reduce-scatter.3.cloned.1.call-start
  11.1 57.1 %all-gather.5.cloned.1.call-done = bf16[512,4096]{1,0:T(8,128)(2,1)} async-done(((bf16[512,512]{1,0:T(8,128)(2,1)}), bf16[512,4096]{1,0:T(8,128)(2,1)}) %all-gather.5.cloned.1.call-update) | async-done | bytes 4194320 | tf_op jit(solution)/shard_map/all_gather | solution.py:31
  68.2 3.1 multiply_reduce_fusion
  71.2 85.9 %all-gather.3.cloned.1.call-done = bf16[512,4096]{1,0:T(8,128)(2,1)} async-done(((bf16[512,128]{1,0:T(8,128)(2,1)}), bf16[512,4096]{1,0:T(8,128)(2,1)}) %all-gather.3.cloned.1.call-update) | async-done | bytes 4194320 | tf_op jit(solution)/shard_map/all_gather | solution.py:39
  157.1 0.0 copy-start
  157.1 3.2 multiply_reduce_fusion.1
  160.3 0.2 copy-done
  160.6 4.7 fusion.2
  165.3 59.4 %pmax.42 = f32[512]{0:T(512)S(1)} all-reduce(f32[512]{0:T(512)S(1)} %get-tuple-element.5), channel_id=1, replica_groups=mesh['row'=8,'col'=32] {'col'}, use_global_device_ids=true, to_apply=%region_3.0 | all-reduce | flops 512 | bytes 4096 | tf_op jit(solution)/shard_map/pmax | solution.py:16
  224.7 0.3 exponential_reduce_fusion.5
  225.0 65.0 %psum.56 = f32[512]{0:T(512)S(1)} all-reduce(f32[512]{0:T(512)S(1)} %exponential_reduce_fusion.5), channel_id=1, replica_groups=mesh['row'=8,'col'=32] {'col'}, use_global_device_ids=true, to_apply=%region_5.0 | all-reduce | flops 512 | bytes 4096 | tf_op jit(solution)/shard_map/psum | solution.py:17
  290.1 0.2 fusion.3
  290.2 19.6 %pmax.43 = f32[512]{0:T(512)S(1)} all-reduce(f32[512]{0:T(512)S(1)} %fusion.3), channel_id=1, replica_groups=mesh['row'=8,'col'=32] {'row'}, use_global_device_ids=true, to_apply=%region_7.0 | all-reduce | flops 512 | bytes 4096 | tf_op jit(solution)/shard_map/pmax | solution.py:23
  309.8 0.3 exponential_reduce_fusion.4
  310.1 16.0 %psum.57 = f32[512]{0:T(512)S(1)} all-reduce(f32[512]{0:T(512)S(1)} %exponential_reduce_fusion.4), channel_id=1, replica_groups=mesh['row'=8,'col'=32] {'row'}, use_global_device_ids=true, to_apply=%region_9.0 | all-reduce | flops 512 | bytes 4096 | tf_op jit(solution)/shard_map/psum | solution.py:24
  326.1 0.2 fusion.4
  326.3 65.0 %pmax.44 = f32[512]{0:T(512)S(1)} all-reduce(f32[512]{0:T(512)S(1)} %fusion.4), channel_id=1, replica_groups=mesh['row'=8,'col'=32] {'col'}, use_global_device_ids=true, to_apply=%region_11.0 | all-reduce | flops 512 | bytes 4096 | tf_op jit(solution)/shard_map/pmax | solution.py:16
  391.3 0.3 exponential_reduce_fusion.3
  391.7 65.0 %psum.58 = f32[512]{0:T(512)S(1)} all-reduce(f32[512]{0:T(512)S(1)} %exponential_reduce_fusion.3), channel_id=1, replica_groups=mesh['row'=8,'col'=32] {'col'}, use_global_device_ids=true, to_apply=%region_13.0 | all-reduce | flops 512 | bytes 4096 | tf_op jit(solution)/shard_map/psum | solution.py:17
  456.7 0.2 fusion.5
  456.9 17.9 %pmax.45 = f32[512]{0:T(512)S(1)} all-reduce(f32[512]{0:T(512)S(1)} %fusion.5), channel_id=1, replica_groups=mesh['row'=8,'col'=32] {'row'}, use_global_device_ids=true, to_apply=%region_15.0 | all-reduce | flops 512 | bytes 4096 | tf_op jit(solution)/shard_map/pmax | solution.py:23
  474.8 0.3 exponential_reduce_fusion.2
  475.1 16.0 %psum.59 = f32[512]{0:T(512)S(1)} all-reduce(f32[512]{0:T(512)S(1)} %exponential_reduce_fusion.2), channel_id=1, replica_groups=mesh['row'=8,'col'=32] {'row'}, use_global_device_ids=true, to_apply=%region_17.0 | all-reduce | flops 512 | bytes 4096 | tf_op jit(solution)/shard_map/psum | solution.py:24
  491.1 0.2 fusion.6
  491.3 65.0 %pmax.46 = f32[512]{0:T(512)S(1)} all-reduce(f32[512]{0:T(512)S(1)} %fusion.6), channel_id=1, replica_groups=mesh['row'=8,'col'=32] {'col'}, use_global_device_ids=true, to_apply=%region_19.0 | all-reduce | flops 512 | bytes 4096 | tf_op jit(solution)/shard_map/pmax | solution.py:16
  556.3 0.3 exponential_reduce_fusion.1
  556.7 65.0 %psum.60 = f32[512]{0:T(512)S(1)} all-reduce(f32[512]{0:T(512)S(1)} %exponential_reduce_fusion.1), channel_id=1, replica_groups=mesh['row'=8,'col'=32] {'col'}, use_global_device_ids=true, to_apply=%region_21.0 | all-reduce | flops 512 | bytes 4096 | tf_op jit(solution)/shard_map/psum | solution.py:17
  621.7 0.2 fusion.7
  621.9 17.9 %pmax.47 = f32[512]{0:T(512)S(1)} all-reduce(f32[512]{0:T(512)S(1)} %fusion.7), channel_id=1, replica_groups=mesh['row'=8,'col'=32] {'row'}, use_global_device_ids=true, to_apply=%region_23.0 | all-reduce | flops 512 | bytes 4096 | tf_op jit(solution)/shard_map/pmax | solution.py:23
  639.8 0.3 exponential_reduce_fusion
  640.1 16.0 %psum.61 = f32[512]{0:T(512)S(1)} all-reduce(f32[512]{0:T(512)S(1)} %exponential_reduce_fusion), channel_id=1, replica_groups=mesh['row'=8,'col'=32] {'row'}, use_global_device_ids=true, to_apply=%region_25.0 | all-reduce | flops 512 | bytes 4096 | tf_op jit(solution)/shard_map/psum | solution.py:24
  656.1 0.5 convert_reduce_fusion
  656.6 7.8 fusion.8
  664.3 0.0 reduce-scatter.3.cloned.1.call-update
  664.3 0.2 reduce-scatter.5.cloned.1.call-start
  664.6 7.8 fusion.9
  672.3 0.0 reduce-scatter.5.cloned.1.call-update
  672.4 65.2 %psum.62 = f32[512]{0:T(512)S(1)} all-reduce(f32[512]{0:T(512)S(1)} %get-tuple-element.3), channel_id=1, replica_groups=mesh['row'=8,'col'=32] {'col'}, use_global_device_ids=true, to_apply=%region_28.0 | all-reduce | flops 512 | bytes 4096 | tf_op jit(solution)/shard_map/psum | solution.py:55
  737.6 0.1 dynamic_slice.3
  737.7 18.0 %psum.63 = f32[512]{0:T(512)S(1)} all-reduce(f32[512]{0:T(512)S(1)} %get-tuple-element.2), channel_id=1, replica_groups=mesh['row'=8,'col'=32] {'row'}, use_global_device_ids=true, to_apply=%region_31.0 | all-reduce | flops 512 | bytes 4096 | tf_op jit(solution)/shard_map/psum | solution.py:56
  755.7 65.2 %reduce-scatter.3.cloned.1.call-done = f32[16,4096]{1,0:T(8,128)} async-done(((f32[512,4096]{1,0:T(8,128)}), f32[16,4096]{1,0:T(8,128)}) %reduce-scatter.3.cloned.1.call-update) | async-done | bytes 262160 | tf_op jit(solution)/shard_map/reduce_scatter | solution.py:58
  820.9 1.7 broadcast_divide_fusion.1
  822.6 94.9 %reduce-scatter.5.cloned.1.call-done = f32[512,512]{1,0:T(8,128)} async-done(((f32[512,4096]{1,0:T(8,128)}), f32[512,512]{1,0:T(8,128)}) %reduce-scatter.5.cloned.1.call-update) | async-done | bytes 1048592 | tf_op jit(solution)/shard_map/reduce_scatter | solution.py:69
  917.5 2.3 broadcast_divide_fusion
  (6 shorter events, 0.1 us)
Async XLA Ops:
  7.2 61.0 %all-gather.5.cloned.1.call-start = ((), (), s32[]{:S(2)}) async-start(), calls=%async_computation.3 | async-start | bytes 4718592 | tf_op jit(solution)/shard_map/all_gather | solution.py:31
  9.3 147.8 %all-gather.3.cloned.1.call-start = ((), (), s32[]{:S(2)}) async-start(), calls=%async_computation.2 | async-start | bytes 4325376 | tf_op jit(solution)/shard_map/all_gather | solution.py:39
  11.0 809.8 %reduce-scatter.3.cloned.1.call-start = ((), (), s32[]{:S(2)}) async-start(), calls=%async_computation.4 | async-start | bytes 8650752 | tf_op jit(solution)/shard_map/reduce_scatter | solution.py:58
  157.1 3.4 copy-start
  664.3 253.2 %reduce-scatter.5.cloned.1.call-start = ((), (), s32[]{:S(2)}) async-start(), calls=%async_computation.5 | async-start | bytes 9437184 | tf_op jit(solution)/shard_map/reduce_scatter | solution.py:69
Sparse Core Ops, SparseCore 0:
  10.4 57.7 all-gather.4
  71.3 85.7 all-gather.2
  664.5 156.3 reduce-scatter.2
  823.3 94.2 reduce-scatter.4
where the time goes:
time: 928 us; the launch traced here: 926 us
  blocking collectives  571 us (62%)
  waiting for transfers between devices  303 us (33%)
  matrix products  20.3 us (2%)
  other arithmetic  17.4 us (2%)
  between operations  13.8 us (1%)
    psum x3, blocking collectives, row_softmin(): lax.psum(jnp.sum(jnp.exp(scores - largest[:, None]), axis=1), 'col')  195 us
    pmax x3, blocking collectives, row_softmin(): largest = lax.pmax(local_max, 'col')  189 us
    reduce_scatter x1, waiting for transfers between devices, local(): lax.psum_scatter(data_partial, 'row', scatter_dimension=1, tiled=True)  94.9 us
    all_gather x1, waiting for transfers between devices, local(): noise_block = lax.all_gather(noise_half, 'col', axis=1, tiled=True)  85.9 us
    psum x1, blocking collectives, local(): row_mass = lax.psum(jnp.sum(coupling.astype(jnp.float32), axis=1), 'col')  65.2 us
    reduce_scatter x1, waiting for transfers between devices, local(): lax.psum_scatter(jnp.dot(coupling, data_block, preferred_element_type=jnp...  65.2 us
    all_gather x1, waiting for transfers between devices, local(): data_block = lax.all_gather(data_half, 'row', axis=1, tiled=True)  57.1 us
    pmax x3, blocking collectives, col_softmin(): largest = lax.pmax(local_max, 'row')  55.5 us
  transfers between devices with their start and end apart: 4, of which 4 were waited for; matrix products, arithmetic and copies ran while one was open for 2% of the time, Pallas kernels for 0%

commit v1 on v0

v1 whole, which is shorter than its diff:
```python
import functools
import math

import jax
import jax.numpy as jnp
from jax import lax
from jax.experimental import pallas as pl
from jax.experimental.pallas import tpu as pltpu
from jax.sharding import PartitionSpec as P

ITERS = 3
YN = 4
ROWS = 8
MESH = pl.DeviceIdType.MESH
F32 = jnp.float32
BF16 = jnp.bfloat16
NT = (((1,), (1,)), ((), ()))
NN = (((1,), (0,)), ((), ()))


def remote(src, dst, send, recv, **dev):
    return pltpu.make_async_remote_copy(
        src_ref=src, dst_ref=dst, send_sem=send, recv_sem=recv,
        device_id=dev, device_id_type=MESH,
    )


def landed(ref, sem):
    pltpu.make_async_copy(ref, ref, sem).wait()


def column(rows4):
    blocks = [
        jnp.transpose(jnp.broadcast_to(rows4[k:k + 1, :], (128, 128)))
        for k in range(rows4.shape[0])
    ]
    return jnp.concatenate(blocks, axis=0)


def local_lse(mat, col, out):
    q = mat.shape[1] // 128
    for k in range(q):
        x = col[...] - mat[:, k * 128:(k + 1) * 128]
        m = jnp.max(x, axis=0, keepdims=True)
        s = jnp.sum(jnp.exp2(x - m), axis=0, keepdims=True)
        out[k:k + 1, :] = m
        out[q + k:q + k + 1, :] = s


def combine(parts):
    q = parts.shape[1] // 2
    m = parts[:, :q, :]
    s = parts[:, q:, :]
    top = jnp.max(m, axis=0)
    return top, jnp.sum(s * jnp.exp2(m - top[None]), axis=0)


def kernel(
    cfg, noise_ref, data_ref, nt_ref, dt_ref,
    noise_f, data_f, s_nm, s_mn, c_nm, c_mn, u_col, v_col, sq_n, sq_m, u_row, v_row,
    core_x, col_x, row_x,
    p_b, rb3, rb_half, rb4, rb5, q_b, q_r, q_s, z_first, z_next, h_out, h_in, own,
    nsend, nrecv, dsend, drecv,
    core_send, core_recv, col_send, col_recv, row_send, row_recv,
    psend, precv, qsend, qrecv, zsend, zrecv,
):
    zn, stage = cfg
    nb = noise_ref.shape[0]
    mb = data_ref.shape[0]
    kd = data_ref.shape[1]
    kn = noise_ref.shape[1]
    cols = 4 * zn
    npp = cols // ROWS
    zh_n = 2 * zn
    half = mb // 2
    features = kd * ROWS
    scale = math.log2(math.e) / (0.25 * features)
    log_rows = math.log2(nb * ROWS)
    log_cols = math.log2(mb * cols)

    row = lax.axis_index("row")
    col = lax.axis_index("col")
    xl = lax.div(row, YN)
    y = lax.rem(row, YN)
    z = lax.div(col, 4)
    h = lax.rem(lax.div(col, 2), 2)
    c = lax.rem(col, 2)

    def rid(dx, dy):
        return lax.rem(xl + dx, 2) * YN + lax.rem(y + dy, YN)

    def zz(d):
        return lax.rem(z + d + zn, zn)

    def cid(zi, hi, ci):
        return (zi * 2 + hi) * 2 + ci

    y_up, y_dn, x_p = rid(0, 1), rid(0, 3), rid(1, 0)
    z_up, z_dn = cid(zz(1), h, c), cid(zz(-1), h, c)
    h_p = cid(z, 1 - h, c)
    c_p = cid(z, h, 1 - c)
    zh = z * 2 + h

    noise_f[col] = noise_ref[...].astype(BF16)
    data_f[row] = data_ref[...].astype(BF16)

    barrier = pltpu.get_barrier_semaphore()

    def greet(**dev):
        pl.semaphore_signal(barrier, inc=1, device_id=dev, device_id_type=MESH)

    for d in range(1, ROWS):
        greet(row=lax.rem(row + d, ROWS))
    greet(col=c_p)
    for d in range(1, zh_n):
        greet(col=lax.rem(zh + d, zh_n) * 2 + c)
    pl.semaphore_wait(barrier, ROWS - 1 + 1 + zh_n - 1)

    pending = []
    n_count = [0]
    d_count = [0]

    def send_noise(piece, dev):
        k = n_count[0]
        n_count[0] += 1
        cp = remote(noise_f.at[piece], noise_f.at[piece], nsend.at[k], nrecv.at[piece], col=dev)
        cp.start()
        pending.append(cp)

    def got_noise(piece):
        landed(noise_f.at[piece], nrecv.at[piece])

    def data_half(r, i):
        return data_f.at[r, pl.ds(i * half, half), :]

    def send_data(r, i, dev):
        k = d_count[0]
        d_count[0] += 1
        cp = remote(data_half(r, i), data_half(r, i), dsend.at[k], drecv.at[r, i], row=dev)
        cp.start()
        pending.append(cp)

    def got_data(r, i):
        landed(data_half(r, i), drecv.at[r, i])

    send_noise(col, z_up)
    send_noise(col, z_dn)
    send_noise(col, h_p)
    send_noise(col, c_p)
    for i in (0, 1):
        send_data(row, i, y_up)
        send_data(row, 1 - i, y_dn)
        send_data(row, i, x_p)

    zhalf = zn // 2

    def noise_step(s):
        if s < zhalf:
            for hi in (h, 1 - h):
                up, dn = cid(zz(-s), hi, c), cid(zz(s), hi, c)
                got_noise(up)
                if s < zhalf - 1:
                    send_noise(up, z_up)
                send_noise(up, c_p)
                got_noise(dn)
                if s < zhalf - 1:
                    send_noise(dn, z_dn)
                send_noise(dn, c_p)
            if s == zhalf - 1:
                send_noise(cid(zz(-s), 0, c), z_up)
                send_noise(cid(zz(s), 1, c), z_dn)
        else:
            far = zz(zhalf)
            for hi in (0, 1):
                got_noise(cid(far, hi, c))
                send_noise(cid(far, hi, c), c_p)

    got_noise(h_p)
    if zhalf > 1:
        send_noise(h_p, z_up)
        send_noise(h_p, z_dn)
    else:
        raise NotImplementedError
    send_noise(h_p, c_p)
    noise_step(1)
    got_data(y_dn, 0)
    send_data(y_dn, 0, y_up)
    got_data(y_up, 1)
    send_data(y_up, 1, y_dn)
    got_data(x_p, 0)
    send_data(x_p, 0, y_up)
    send_data(x_p, 0, y_dn)
    if zhalf > 2:
        noise_step(2)
    got_data(x_p, 1)
    send_data(x_p, 1, y_up)
    send_data(x_p, 1, y_dn)
    for i in (0, 1):
        got_data(rid(0, 2), i)
        send_data(rid(0, 2), i, x_p)
    for s in range(3, zhalf + 1):
        noise_step(s)
    if zhalf == 2:
        noise_step(2)
    for zi in range(zn):
        for hi in (0, 1):
            got_noise(cid(zi, hi, 1 - c))
    got_data(y_dn, 1)
    got_data(y_up, 0)

    s_nm[...] = jnp.zeros_like(s_nm)
    s_mn[...] = jnp.zeros_like(s_mn)
    sq_n[...] = jnp.zeros_like(sq_n)
    sq_m[...] = jnp.zeros_like(sq_m)

    def noise_cat(r):
        return jnp.concatenate([noise_f[r * npp + i] for i in range(npp)], axis=1)

    def chunk(r):
        a = noise_cat(r)
        d = data_f[r]
        s_nm[...] += lax.dot_general(a, d, NT, preferred_element_type=F32)
        s_mn[...] += lax.dot_general(d, a, NT, preferred_element_type=F32)
        for sq, v in ((sq_n, a), (sq_m, d)):
            total = sq[...]
            for i in range(v.shape[1] // 128):
                w = v[:, i * 128:(i + 1) * 128].astype(F32)
                total += w * w
            sq[...] = total

    def first(k, carry):
        dx = jnp.where(k == 3, 1, 0)
        dy = jnp.where(k == 1, 1, jnp.where(k == 2, 3, jnp.where(k == 4, 2, 0)))
        chunk(rid(dx, dy))
        return carry

    lax.fori_loop(0, 5, first, 0)

    def last(k, carry):
        dy = jnp.where(k == 0, 1, jnp.where(k == 1, 3, 2))
        r = rid(1, dy)
        got_data(r, 0)
        got_data(r, 1)
        chunk(r)
        return carry

    lax.fori_loop(0, 3, last, 0)

    def rows_of(sq):
        t = jnp.sum(jnp.transpose(sq), axis=0, keepdims=True)
        return jnp.concatenate([t[:, k * 128:(k + 1) * 128] for k in range(t.shape[1] // 128)], axis=0)

    ns = rows_of(sq_n[...])
    ds = rows_of(sq_m[...])
    u_col[...] = column(ns)
    v_col[...] = column(ds)
    for k in range(mb // 128):
        at = (slice(None), slice(k * 128, (k + 1) * 128))
        s_nm[at] = (u_col[...] + ds[k:k + 1, :] - 2.0 * s_nm[at]) * scale
    for k in range(nb // 128):
        at = (slice(None), slice(k * 128, (k + 1) * 128))
        s_mn[at] = (v_col[...] + ns[k:k + 1, :] - 2.0 * s_mn[at]) * scale

    def start_core(t):
        cp = remote(core_x.at[t, c], core_x.at[t, c], core_send.at[t], core_recv.at[t], col=c_p)
        cp.start()
        pending.append(cp)

    def start_col(t):
        for d in range(1, zh_n):
            remote(col_x.at[t, zh], col_x.at[t, zh], col_send.at[t], col_recv.at[t],
                   col=lax.rem(zh + d, zh_n) * 2 + c).start()

    def start_row(t):
        for d in range(1, ROWS):
            remote(row_x.at[t, row], row_x.at[t, row], row_send.at[t], row_recv.at[t],
                   row=lax.rem(row + d, ROWS)).start()

    def got_col(t):
        landed(col_x.at[t, pl.ds(0, zh_n - 1)], col_recv.at[t])

    def got_row(t):
        landed(row_x.at[t, pl.ds(0, ROWS - 1)], row_recv.at[t])

    if stage >= 2:
        v_col[...] = jnp.zeros_like(v_col)
        qn, qm = nb // 128, mb // 128
        for t in range(ITERS):
            local_lse(s_mn, v_col, core_x.at[t, c])
            start_core(t)
            landed(core_x.at[t, 1 - c], core_recv.at[t])
            top, total = combine(core_x[t])
            col_x[t, zh, 0:qn, :] = top
            col_x[t, zh, qn:2 * qn, :] = total
            start_col(t)
            got_col(t)
            top, total = combine(col_x[t])
            u = -(top + jnp.log2(total) + log_rows)
            u_row[...] = u
            u_col[...] = column(u)
            local_lse(s_nm, u_col, row_x.at[t, row])
            start_row(t)
            got_row(t)
            top, total = combine(row_x[t])
            v = -(top + jnp.log2(total) + log_cols)
            v_row[...] = v
            v_col[...] = column(v)

    if stage >= 3:
        t = ITERS
        logs = log_rows + log_cols
        core_x[t, c] = jnp.zeros(core_x.shape[2:], F32)
        row_x[t, row] = jnp.zeros(row_x.shape[2:], F32)
        for k in range(nb // 128):
            at = (slice(None), slice(k * 128, (k + 1) * 128))
            w = jnp.exp2(v_col[...] + u_row[k:k + 1, :] - s_mn[at] + logs).astype(BF16)
            c_mn[at] = w
            core_x[t, c, k:k + 1, :] = jnp.sum(w.astype(F32), axis=0, keepdims=True)
        start_core(t)

        def p_dot(r):
            return lax.dot_general(c_mn[...], noise_cat(r), NN, preferred_element_type=F32)

        def lead(k, carry):
            r = rid(1, jnp.where(k == 0, 2, jnp.where(k == 1, 1, 3)))
            dev = jnp.where(k == 0, x_p, jnp.where(k == 1, y_up, y_dn))
            p_b[r] = p_dot(r).astype(BF16)
            remote(p_b.at[r], rb3.at[k], psend.at[k], precv.at[k], row=dev).start()
            return carry

        lax.fori_loop(0, 3, lead, 0)

        for k in range(mb // 128):
            at = (slice(None), slice(k * 128, (k + 1) * 128))
            w = jnp.exp2(u_col[...] + v_row[k:k + 1, :] - s_nm[at] + logs).astype(BF16)
            c_nm[at] = w
            row_x[t, row, k:k + 1, :] = jnp.sum(w.astype(F32), axis=0, keepdims=True)
        start_row(t)

        def lanes(r):
            return pl.ds(pl.multiple_of(r * kd, kd), kd)

        share = nb // cols

        def q_loop(r, carry):
            w = lax.dot_general(c_nm[...], data_f[r], NN, preferred_element_type=F32)
            q_b[:, :, :, lanes(r)] = w.astype(BF16).reshape(zh_n, 2, share, kd)
            remote(q_b.at[:, 1 - c, :, lanes(r)], q_r.at[:, :, lanes(r)],
                   qsend.at[r], qrecv.at[r], col=c_p).start()
            return carry

        lax.fori_loop(0, ROWS, q_loop, 0)

        def q_sum(r, carry):
            landed(q_r.at[:, :, lanes(r)], qrecv.at[r])
            q_s[:, :, lanes(r)] = (
                q_b[:, c, :, lanes(r)].astype(F32) + q_r[:, :, lanes(r)].astype(F32)
            ).astype(BF16)
            return carry

        lax.fori_loop(0, ROWS, q_sum, 0)

        landed(core_x.at[t, 1 - c], core_recv.at[t])
        col_x[t, zh] = core_x[t, 0] + core_x[t, 1]
        start_col(t)

        z_count = [0]

        def z_send(src, dst, sem, dev):
            k = z_count[0]
            z_count[0] += 1
            cp = remote(src, dst, zsend.at[k], zrecv.at[sem], col=dev)
            cp.start()
            pending.append(cp)

        far = zz(zhalf)
        z_send(q_s.at[far * 2], z_first.at[0], 0, z_up)
        z_send(q_s.at[far * 2 + 1], z_first.at[1], 1, z_dn)

        def rest(k, carry):
            dx = jnp.where(k == 1, 1, 0)
            dy = jnp.where(k == 0, 2, jnp.where(k == 2, 1, jnp.where(k == 3, 3, 0)))
            r = rid(dx, dy)
            p_b[r] = p_dot(r).astype(BF16)
            return carry

        lax.fori_loop(0, 5, rest, 0)

        def z_step(s):
            for i, sign, dev in ((0, 1, z_up), (1, -1, z_dn)):
                dest = zz(sign * (zhalf - s))
                if s == 1:
                    landed(z_first.at[i], zrecv.at[i])
                    q_s[dest * 2 + i] = (q_s[dest * 2 + i].astype(F32) + z_first[i].astype(F32)).astype(BF16)
                else:
                    landed(z_next.at[s - 2, i], zrecv.at[2 * (s - 1) + i])
                    two = pl.ds(dest * 2, 2)
                    q_s[two] = (q_s[two].astype(F32) + z_next[s - 2, i].astype(F32)).astype(BF16)
                z_send(q_s.at[pl.ds(dest * 2, 2)], z_next.at[s - 1, i], 2 * s + i, dev)

        z_step(1)

        def add_to(r, i, ref):
            at = pl.ds(i * half, half)
            p_b[r, at, :] = (p_b[r, at, :].astype(F32) + ref.astype(F32)).astype(BF16)

        def p_send(k, src, dst, dev):
            cp = remote(src, dst, psend.at[k], precv.at[k], row=dev)
            cp.start()
            pending.append(cp)

        landed(rb3.at[0], precv.at[0])
        r2 = rid(0, 2)
        add_to(r2, 0, rb3[0, :half])
        p_send(3, p_b.at[r2, pl.ds(0, half), :], rb_half.at[0], y_up)
        add_to(r2, 1, rb3[0, half:])
        p_send(4, p_b.at[r2, pl.ds(half, half), :], rb_half.at[1], y_dn)
        landed(rb3.at[1], precv.at[1])
        landed(rb3.at[2], precv.at[2])
        p_b[x_p] = (p_b[x_p].astype(F32) + rb3[1].astype(F32) + rb3[2].astype(F32)).astype(BF16)
        p_send(5, p_b.at[x_p], rb4, x_p)
        if zhalf > 2:
            z_step(2)
        landed(rb_half.at[0], precv.at[3])
        add_to(y_up, 0, rb_half[0])
        p_send(6, p_b.at[y_up], rb5.at[0], y_up)
        landed(rb_half.at[1], precv.at[4])
        add_to(y_dn, 1, rb_half[1])
        p_send(7, p_b.at[y_dn], rb5.at[1], y_dn)
        for s in range(3, zhalf):
            z_step(s)

        for i in (0, 1):
            landed(z_next.at[zhalf - 2, i], zrecv.at[2 * (zhalf - 1) + i])
        mine = q_s[pl.ds(z * 2, 2)].astype(F32) + z_next[zhalf - 2, 0].astype(F32) + z_next[zhalf - 2, 1].astype(F32)
        own[...] = mine
        h_out[...] = own[1 - h].astype(BF16)
        z_send(h_out, h_in, 2 * zhalf, h_p)

        got_row(t)
        qm = mb // 128
        col_mass = jnp.sum(row_x[t], axis=0)[:qm]
        v_col[...] = column(1.0 / col_mass)
        got_col(t)
        qn = nb // 128
        row_mass = jnp.sum(col_x[t], axis=0)[:qn]
        u_col[...] = column(1.0 / row_mass)

        landed(rb4, precv.at[5])
        landed(rb5.at[0], precv.at[6])
        landed(rb5.at[1], precv.at[7])
        for k in range(kd // 128):
            at = slice(k * 128, (k + 1) * 128)
            dt_ref[:, at] = v_col[...] * (
                p_b[row, :, at].astype(F32) + rb4[:, at].astype(F32)
                + rb5[0, :, at].astype(F32) + rb5[1, :, at].astype(F32)
            )
        landed(h_in, zrecv.at[2 * zhalf])
        inv = u_col[pl.ds(pl.multiple_of(col * share, share), share), :]
        for k in range(nt_ref.shape[1] // 128):
            at = slice(k * 128, (k + 1) * 128)
            nt_ref[:, at] = inv * (own[h, :, at] + h_in[:, at].astype(F32))

    for cp in pending:
        cp.wait_send()
    for t in range(ITERS + 1):
        if (stage >= 2 and t < ITERS) or stage >= 3:
            landed(col_x.at[t, pl.ds(0, zh_n - 1)], col_send.at[t])
            landed(row_x.at[t, pl.ds(0, ROWS - 1)], row_send.at[t])
    if stage >= 3:
        for k in range(3):
            landed(rb3.at[k], psend.at[k])

        def left(r, carry):
            landed(q_r.at[:, :, lanes(r)], qsend.at[r])
            return carry

        lax.fori_loop(0, ROWS, left, 0)
    if stage < 3:
        nt_ref[...] = jnp.zeros_like(nt_ref)
        dt_ref[...] = s_nm[...] + s_mn[...]


def local(noise, data, zn, stage=3):
    nb, kn = noise.shape
    mb, kd = data.shape
    cols = 4 * zn
    zh_n = 2 * zn
    features = kd * ROWS
    share = nb // cols
    half = mb // 2
    zhalf = zn // 2
    vm = pltpu.VMEM
    dma = pltpu.SemaphoreType.DMA
    ex = ITERS + 1
    scratch = [
        vm((cols, nb, kn), BF16), vm((ROWS, mb, kd), BF16),
        vm((nb, mb), F32), vm((mb, nb), F32), vm((nb, mb), BF16), vm((mb, nb), BF16),
        vm((nb, 128), F32), vm((mb, 128), F32), vm((nb, 128), F32), vm((mb, 128), F32),
        vm((nb // 128, 128), F32), vm((mb // 128, 128), F32),
        vm((ex, 2, nb // 64, 128), F32), vm((ex, zh_n, nb // 64, 128), F32), vm((ex, ROWS, mb // 64, 128), F32),
        vm((ROWS, mb, kd), BF16), vm((3, mb, kd), BF16), vm((2, half, kd), BF16),
        vm((mb, kd), BF16), vm((2, mb, kd), BF16),
        vm((zh_n, 2, share, features), BF16), vm((zh_n, share, features), BF16), vm((zh_n, share, features), BF16),
        vm((2, share, features), BF16), vm((zhalf - 1, 2, 2, share, features), BF16),
        vm((share, features), BF16), vm((share, features), BF16), vm((2, share, features), F32),
        dma((40,)), dma((cols,)), dma((16,)), dma((ROWS, 2)),
        dma((ex,)), dma((ex,)), dma((ex,)), dma((ex,)), dma((ex,)), dma((ex,)),
        dma((8,)), dma((8,)), dma((ROWS,)), dma((ROWS,)), dma((2 * zhalf + 1,)), dma((2 * zhalf + 1,)),
    ]
    return pl.pallas_call(
        functools.partial(kernel, (zn, stage)),
        out_shape=(
            jax.ShapeDtypeStruct((share, features), F32),
            jax.ShapeDtypeStruct((mb, kd), F32),
        ),
        in_specs=[pl.BlockSpec(memory_space=pltpu.VMEM)] * 2,
        out_specs=[pl.BlockSpec(memory_space=pltpu.VMEM)] * 2,
        scratch_shapes=scratch,
        compiler_params=pltpu.CompilerParams(
            collective_id=0, has_side_effects=True, vmem_limit_bytes=56 * 1024 * 1024
        ),
    )(noise, data)


def solution(mesh, stage=3):
    zn = mesh.shape["col"] // 4
    return jax.shard_map(
        functools.partial(local, zn=zn, stage=stage),
        mesh=mesh,
        in_specs=(P("row", "col"), P("col", "row")),
        out_specs=(P(("row", "col"), None), P("col", "row")),
        check_vma=False,
    )
```

time: 928 us -> 129 us (0.14)
  blocking collectives: 571 us -> 0 us
  waiting for transfers between devices: 303 us -> 0 us
  Pallas kernels: 0 us -> 124 us
  matrix products: 20.3 us -> 0 us
  other arithmetic: 17.4 us -> 0 us
  between operations: 13.8 us -> 0.64 us
    psum x8 -> x0, blocking collectives: 326 us -> none  [the longest x3 195 us: row_softmin(): lax.psum(jnp.sum(jnp.exp(scores - largest[:, None]), axis=1), 'col')]
    pmax x6 -> x0, blocking collectives: 245 us -> none  [the longest x3 189 us: row_softmin(): largest = lax.pmax(local_max, 'col')]
    reduce_scatter x2 -> x0, waiting for transfers between devices: 160 us -> none  [the longest x1 94.9 us: local(): lax.psum_scatter(data_partial, 'row', scatter_dimension=1, tiled=True)]
    all_gather x2 -> x0, waiting for transfers between devices: 143 us -> none  [the longest x1 85.9 us: local(): noise_block = lax.all_gather(noise_half, 'col', axis=1, tiled=True)]
    pallas_call x0 -> x1, Pallas kernels: none -> 124 us  [local(): pl.pallas_call(functools.partial(kernel, (zn, stage)), out_shape=(jax.Sha...]
    dot_general x3 -> x0, matrix products: 20.3 us -> none  [the longest x1 7.78 us: local(): jnp.einsum('nm,nk->mk', coupling, noise_block, preferred_element_type=jnp...]
  transfers between devices with their start and end apart: 4 -> 0, of which waited for: 4 -> 0; matrix products, arithmetic and copies ran while one was open for 2% -> 0% of each run, Pallas kernels for 0% -> 0%
where the time goes in v1:
time: 129 us
  Pallas kernels  124 us (96%)
  local copies, waits for them, and re-layouts  3.93 us (3%)
    pallas_call x1, Pallas kernels, local(): pl.pallas_call(functools.partial(kernel, (zn, stage)), out_shape=(jax.Sha...  124 us
    unnamed x2, local copies, waits for them, and re-layouts  3.93 us

profile of v1, /device:TPU:32, one launch (start us, length us, event | category | flops | bytes accessed | tf_op | source)
XLA Modules:
  0.0 128.7 jit_solution(4321682900978872264)
XLA Ops:
  0.6 124.1 %shard_map.41 = (f32[16,4096]{1,0:T(8,128)}, f32[512,512]{1,0:T(8,128)}) custom-call(f32[512,128]{1,0:T(8,128)} %noise_ref.1, f32[512,512]{1,0:T(8,128)} %data_ref.1), custom_call_target="tpu_custom_call" | custom-call | tf_op jit(solution)/shard_map/pallas_call | solution.py:511
  124.8 1.7 %copy.6 = f32[16,4096]{1,0:T(8,128)} copy(f32[16,4096]{1,0:T(8,128)} %get-tuple-element.4) | data formatting | bytes 524288
  126.4 2.3 %copy.7 = f32[512,512]{1,0:T(8,128)} copy(f32[512,512]{1,0:T(8,128)} %get-tuple-element.5) | data formatting | bytes 2097152

commit v2 on v1

v2 whole, which is shorter than its diff:
```python
import functools
import math

import jax
import jax.numpy as jnp
from jax import lax
from jax.experimental import pallas as pl
from jax.experimental.pallas import tpu as pltpu
from jax.sharding import PartitionSpec as P

ITERS = 3
YN = 4
ROWS = 8
ZN = 8
PARTS = 4
MESH = pl.DeviceIdType.MESH
F32 = jnp.float32
BF16 = jnp.bfloat16
NT = (((1,), (1,)), ((), ()))
NN = (((1,), (0,)), ((), ()))


def remote(src, dst, send, recv, **dev):
    return pltpu.make_async_remote_copy(
        src_ref=src, dst_ref=dst, send_sem=send, recv_sem=recv,
        device_id=dev, device_id_type=MESH,
    )


def landed(ref, sem):
    pltpu.make_async_copy(ref, ref, sem).wait()


def column(rows4):
    blocks = [
        jnp.transpose(jnp.broadcast_to(rows4[k:k + 1, :], (128, 128)))
        for k in range(rows4.shape[0])
    ]
    return jnp.concatenate(blocks, axis=0)


def local_lse(mat, col, out):
    for k in range(mat.shape[1] // 128):
        x = col[...] - mat[:, k * 128:(k + 1) * 128]
        m = jnp.max(x, axis=0, keepdims=True)
        s = jnp.sum(jnp.exp2(x - m), axis=0, keepdims=True)
        out[k:k + 1, :] = m + jnp.log2(s)


def combine(parts):
    top = jnp.max(parts, axis=0)
    return top + jnp.log2(jnp.sum(jnp.exp2(parts - top[None]), axis=0))


def kernel(
    cfg, noise_ref, data_ref, nt_ref, dt_ref,
    noise_f, data_f, s_nm, s_mn, c_nm, c_mn, u_col, v_col, sq_n, sq_m, u_row, v_row,
    core_x, col_x, row_x,
    p_b, p_lead, p_half, p_x, p_next, q_b, q_r, q_s, z_first, z_next, h_out, h_in, own,
    nsend, nrecv, dsend, drecv,
    core_send, core_recv, col_send, col_recv, row_send, row_recv,
    psend, precv, p2send, p2recv, qsend, qrecv, zsend, zrecv, hrecv,
):
    stage, opts = cfg
    zn = ZN
    nb = noise_ref.shape[0]
    mb = data_ref.shape[0]
    kd = data_ref.shape[1]
    kn = noise_ref.shape[1]
    cols = 4 * zn
    npp = cols // ROWS
    zh_n = 2 * zn
    half = mb // 2
    part = mb // PARTS
    fold = nb // 2
    features = kd * ROWS
    scale = math.log2(math.e) / (0.25 * features)
    log_rows = math.log2(nb * ROWS)
    log_cols = math.log2(mb * cols)

    row = lax.axis_index("row")
    col = lax.axis_index("col")
    xl = lax.div(row, YN)
    y = lax.rem(row, YN)
    z = lax.div(col, 4)
    h = lax.rem(lax.div(col, 2), 2)
    c = lax.rem(col, 2)

    def rid(dx, dy):
        return lax.rem(xl + dx, 2) * YN + lax.rem(y + dy, YN)

    def zz(d):
        return lax.rem(z + d + zn, zn)

    def cid(zi, hi, ci):
        return (zi * 2 + hi) * 2 + ci

    y_up, y_dn, x_p = rid(0, 1), rid(0, 3), rid(1, 0)
    z_up, z_dn = cid(zz(1), h, c), cid(zz(-1), h, c)
    h_p = cid(z, 1 - h, c)
    c_p = cid(z, h, 1 - c)
    zh = z * 2 + h

    noise_f[col] = noise_ref[...].astype(BF16)
    data_f[row] = data_ref[...].astype(BF16)

    barrier = pltpu.get_barrier_semaphore()

    def greet(**dev):
        pl.semaphore_signal(barrier, inc=1, device_id=dev, device_id_type=MESH)

    for dev in (y_up, y_dn, x_p):
        greet(row=dev)
    for dev in (z_up, z_dn, h_p, c_p):
        greet(col=dev)
    pl.semaphore_wait(barrier, 7)

    pending = []
    n_count = [0]
    d_count = [0]

    def noise_part(piece, i):
        return noise_f.at[piece, pl.ds(i * fold, fold), :]

    def send_noise(piece, i, dev):
        k = n_count[0]
        n_count[0] += 1
        ref = noise_f.at[piece] if i is None else noise_part(piece, i)
        cp = remote(ref, ref, nsend.at[k], nrecv.at[piece, 0 if i is None else i], col=dev)
        cp.start()
        pending.append(cp)

    def got_noise(piece, i):
        ref = noise_f.at[piece] if i is None else noise_part(piece, i)
        landed(ref, nrecv.at[piece, 0 if i is None else i])

    def data_part(r, i):
        return data_f.at[r, pl.ds(i * part, part), :]

    def send_data(r, i, dev):
        k = d_count[0]
        d_count[0] += 1
        cp = remote(data_part(r, i), data_part(r, i), dsend.at[k], drecv.at[r, i], row=dev)
        cp.start()
        pending.append(cp)

    def got_data(r, i):
        landed(data_part(r, i), drecv.at[r, i])

    across = rid(0, 2)
    for i in (0, 1):
        send_noise(col, i, h_p)
        send_noise(col, i, z_up)
        send_noise(col, i, z_dn)
        send_data(row, i, y_up)
        send_data(row, i + 2, y_dn)
        send_data(row, i, x_p)
    send_data(row, 2, y_up)
    send_data(row, 0, y_dn)
    send_data(row, 2, x_p)
    send_data(row, 3, x_p)
    send_noise(col, None, c_p)

    def noise_got(s, hi, i):
        up, dn = cid(zz(-s), hi, c), cid(zz(s), hi, c)
        got_noise(up, i)
        if s < 3 or i == 0:
            send_noise(up, i, z_up)
        got_noise(dn, i)
        if s < 3 or i == 1:
            send_noise(dn, i, z_dn)
        if i == 1:
            send_noise(up, None, c_p)
            send_noise(dn, None, c_p)

    def noise_pair(i):
        got_noise(h_p, i)
        send_noise(h_p, i, z_up)
        send_noise(h_p, i, z_dn)
        if i == 1:
            send_noise(h_p, None, c_p)

    def pass_on(i):
        got_data(y_dn, i)
        send_data(y_dn, i, y_up)
        got_data(y_up, i + 2)
        send_data(y_up, i + 2, y_dn)

    def from_x(i):
        got_data(x_p, i)
        send_data(x_p, i, y_up)
        send_data(x_p, i, y_dn)

    def to_x(i):
        for k in (i, i + 2):
            got_data(across, k)
            send_data(across, k, x_p)

    g = 1 - h
    noise_got(1, h, 0)
    noise_pair(0)
    pass_on(0)
    noise_got(1, h, 1)
    noise_pair(1)
    noise_got(2, h, 0)
    pass_on(1)
    send_data(row, 3, y_up)
    send_data(row, 1, y_dn)
    from_x(0)
    noise_got(2, h, 1)
    noise_got(1, g, 0)
    from_x(1)
    noise_got(3, h, 0)
    noise_got(1, g, 1)
    noise_got(3, h, 1)
    from_x(2)
    to_x(0)
    noise_got(2, g, 0)
    from_x(3)
    to_x(1)
    noise_got(2, g, 1)
    noise_got(3, g, 0)
    noise_got(3, g, 1)
    for i in (2, 3):
        got_data(y_dn, i)
        got_data(y_up, i - 2)

    s_nm[...] = jnp.zeros_like(s_nm)
    s_mn[...] = jnp.zeros_like(s_mn)
    sq_n[...] = jnp.zeros_like(sq_n)
    sq_m[...] = jnp.zeros_like(sq_m)

    def noise_cat(r):
        return jnp.concatenate([noise_f[r * npp + i] for i in range(npp)], axis=1)

    def squares(sq, at, v):
        total = sq[at, :]
        for i in range(v.shape[1] // 128):
            w = v[:, i * 128:(i + 1) * 128].astype(F32)
            total += w * w
        sq[at, :] = total

    def chunk(r, k=None):
        at = pl.ds(0, mb) if k is None else pl.ds(k * half, half)
        a = noise_cat(r)
        d = data_f[r, at, :]
        s_nm[:, at] += lax.dot_general(a, d, NT, preferred_element_type=F32)
        s_mn[at, :] += lax.dot_general(d, a, NT, preferred_element_type=F32)
        squares(sq_m, at, d)
        if k != 1:
            squares(sq_n, pl.ds(0, nb), a)

    def plane(k):
        step = lax.div(k + 1, 2)
        zi = zz(jnp.where(lax.rem(k, 2) == 0, step, -step))
        for hi in (0, 1):
            got_noise(cid(zi, hi, 1 - c), None)

        @pl.when((lax.div(zi, YN) == xl) | (lax.rem(zi, YN) == y))
        def _():
            chunk(zi)

    def near_plane(k, carry):
        plane(k)
        return carry

    lax.fori_loop(0, 5, near_plane, 0)
    far = zz(4)
    for hi in (0, 1):
        for i in (0, 1):
            got_noise(cid(far, hi, c), i)
        send_noise(cid(far, hi, c), None, c_p)
    lax.fori_loop(5, 8, near_plane, 0)

    def sides(k):
        def body(j, carry):
            r = rid(1, jnp.where(j == 0, 1, 3))
            for i in (2 * k, 2 * k + 1):
                got_data(r, i)
            chunk(r, k)
            return carry

        lax.fori_loop(0, 2, body, 0)

    sides(0)
    for i in range(PARTS):
        got_data(rid(1, 2), i)
    chunk(rid(1, 2))
    sides(1)

    def rows_of(sq):
        t = jnp.sum(jnp.transpose(sq), axis=0, keepdims=True)
        return jnp.concatenate([t[:, k * 128:(k + 1) * 128] for k in range(t.shape[1] // 128)], axis=0)

    ns = rows_of(sq_n[...])
    ds = rows_of(sq_m[...])
    u_col[...] = column(ns)
    v_col[...] = column(ds)
    for k in range(mb // 128):
        at = (slice(None), slice(k * 128, (k + 1) * 128))
        s_nm[at] = (u_col[...] + ds[k:k + 1, :] - 2.0 * s_nm[at]) * scale
    for k in range(nb // 128):
        at = (slice(None), slice(k * 128, (k + 1) * 128))
        s_mn[at] = (v_col[...] + ns[k:k + 1, :] - 2.0 * s_mn[at]) * scale

    col_to = [cid(zz(d), hi, c) for d in (4, 3, -3, 2, -2, 1, -1, 0) for hi in (1 - h, h)][:-1]
    row_to = [rid(dx, dy) for dy in (2, 1, 3, 0) for dx in (1, 0)][:-1]

    def start_core(t):
        cp = remote(core_x.at[t, c], core_x.at[t, c], core_send.at[t], core_recv.at[t], col=c_p)
        cp.start()
        pending.append(cp)

    def start_col(t):
        for to in col_to:
            remote(col_x.at[t, zh], col_x.at[t, zh], col_send.at[t], col_recv.at[t], col=to).start()

    def start_row(t):
        for to in row_to:
            remote(row_x.at[t, row], row_x.at[t, row], row_send.at[t], row_recv.at[t], row=to).start()

    def got_col(t):
        landed(col_x.at[t, pl.ds(0, zh_n - 1)], col_recv.at[t])

    def got_row(t):
        landed(row_x.at[t, pl.ds(0, ROWS - 1)], row_recv.at[t])

    if stage >= 2:
        v_col[...] = jnp.zeros_like(v_col)
        for t in range(ITERS):
            local_lse(s_mn, v_col, core_x.at[t, c])
            start_core(t)
            landed(core_x.at[t, 1 - c], core_recv.at[t])
            col_x[t, zh] = combine(core_x[t])
            start_col(t)
            got_col(t)
            u = -(combine(col_x[t]) + log_rows)
            u_row[...] = u
            u_col[...] = column(u)
            local_lse(s_nm, u_col, row_x.at[t, row])
            start_row(t)
            got_row(t)
            v = -(combine(row_x[t]) + log_cols)
            v_row[...] = v
            v_col[...] = column(v)

    wide = features // 2

    def lanes(r):
        return pl.ds(pl.multiple_of(r * kd, kd), kd)

    if stage >= 3:
        t = ITERS
        logs = log_rows + log_cols
        for k in range(nb // 128):
            at = (slice(None), slice(k * 128, (k + 1) * 128))
            w = jnp.exp2(v_col[...] + u_row[k:k + 1, :] - s_mn[at] + logs).astype(BF16)
            c_mn[at] = w
            core_x[t, c, k:k + 1, :] = jnp.sum(w.astype(F32), axis=0, keepdims=True)
        start_core(t)

        def p_dot(r):
            p_b[r] = lax.dot_general(c_mn[...], noise_cat(r), NN, preferred_element_type=F32).astype(BF16)

        def p_half_of(r, i):
            return p_b.at[r, pl.ds(i * half, half), :]

        def lead(k, carry):
            r = rid(1, jnp.where(k == 0, 1, jnp.where(k == 1, 3, 2)))
            dev = jnp.where(k == 0, y_up, jnp.where(k == 1, y_dn, x_p))
            p_dot(r)
            for i in (0, 1):
                remote(p_half_of(r, i), p_lead.at[k, i], psend.at[k, i], precv.at[k, i], row=dev).start()
            return carry

        lax.fori_loop(0, 3, lead, 0)

        for k in range(mb // 128):
            at = (slice(None), slice(k * 128, (k + 1) * 128))
            w = jnp.exp2(u_col[...] + v_row[k:k + 1, :] - s_nm[at] + logs).astype(BF16)
            c_nm[at] = w
            row_x[t, row, k:k + 1, :] = jnp.sum(w.astype(F32), axis=0, keepdims=True)

        share = nb // cols

        def q_loop(r, carry):
            w = lax.dot_general(c_nm[...], data_f[r], NN, preferred_element_type=F32)
            q_b[:, :, :, lanes(r)] = w.astype(BF16).reshape(zh_n, 2, share, kd)
            remote(q_b.at[:, 1 - c, :, lanes(r)], q_r.at[:, :, lanes(r)],
                   qsend.at[r], qrecv.at[r], col=c_p).start()
            return carry

        def q_sum(r, carry):
            landed(q_r.at[:, :, lanes(r)], qrecv.at[r])
            q_s[:, :, lanes(r)] = (
                q_b[:, c, :, lanes(r)].astype(F32) + q_r[:, :, lanes(r)].astype(F32)
            ).astype(BF16)
            return carry

        z_count = [0]

        def z_send(src, dst, sem, dev):
            k = z_count[0]
            z_count[0] += 1
            cp = remote(src, dst, zsend.at[k], sem, col=dev)
            cp.start()
            pending.append(cp)

        def wide_lanes(kk):
            return pl.ds(kk * wide, wide)

        def z_start(kk):
            at = wide_lanes(kk)
            z_send(q_s.at[far * 2, :, at], z_first.at[kk, 0], zrecv.at[kk, 0, 0], z_up)
            z_send(q_s.at[far * 2 + 1, :, at], z_first.at[kk, 1], zrecv.at[kk, 0, 1], z_dn)

        def z_add(s, kk, i, zi):
            ln = wide_lanes(kk)
            if s == 1:
                landed(z_first.at[kk, i], zrecv.at[kk, 0, i])
                at = (zi * 2 + i, slice(None), ln)
                q_s[at] = (q_s[at].astype(F32) + z_first[kk, i].astype(F32)).astype(BF16)
            else:
                landed(z_next.at[s - 2, kk, i], zrecv.at[kk, s - 1, i])
                at = (pl.ds(zi * 2, 2), slice(None), ln)
                q_s[at] = (q_s[at].astype(F32) + z_next[s - 2, kk, i].astype(F32)).astype(BF16)

        def z_step(s, kk):
            for i, sign, dev in ((0, 1, z_up), (1, -1, z_dn)):
                zi = zz(sign * (4 - s))
                z_add(s, kk, i, zi)
                z_send(q_s.at[pl.ds(zi * 2, 2), :, wide_lanes(kk)], z_next.at[s - 1, kk, i], zrecv.at[kk, s, i], dev)

        def z_end(kk):
            ln = wide_lanes(kk)
            for i in (0, 1):
                landed(z_next.at[2, kk, i], zrecv.at[kk, 3, i])
            own[:, :, ln] = (
                q_s[pl.ds(z * 2, 2), :, ln].astype(F32)
                + z_next[2, kk, 0].astype(F32) + z_next[2, kk, 1].astype(F32)
            )
            h_out[kk] = own[1 - h, :, ln].astype(BF16)
            z_send(h_out.at[kk], h_in.at[kk], hrecv.at[kk], h_p)

        def rest(k, carry):
            dx = jnp.where(k == 1, 1, 0)
            dy = jnp.where(k == 0, 2, jnp.where(k == 2, 1, jnp.where(k == 3, 3, 0)))
            p_dot(rid(dx, dy))
            return carry

        def add_to(r, i, ref):
            at = pl.ds(i * half, half)
            p_b[r, at, :] = (p_b[r, at, :].astype(F32) + ref.astype(F32)).astype(BF16)

        p_count = [0]

        def p_send(r, i, dst, sem, dev):
            k = p_count[0]
            p_count[0] += 1
            cp = remote(p_half_of(r, i), dst, p2send.at[k], sem, row=dev)
            cp.start()
            pending.append(cp)

        def opposite(i):
            landed(p_lead.at[2, i], precv.at[2, i])
            add_to(across, i, p_lead[2, i])
            p_send(across, i, p_half.at[i], p2recv.at[i], (y_up, y_dn)[i])

        def over_x(i):
            landed(p_lead.at[0, i], precv.at[0, i])
            landed(p_lead.at[1, i], precv.at[1, i])
            at = (x_p, pl.ds(i * half, half), slice(None))
            p_b[at] = (p_b[at].astype(F32) + p_lead[0, i].astype(F32) + p_lead[1, i].astype(F32)).astype(BF16)
            p_send(x_p, i, p_x.at[i], p2recv.at[2 + i], x_p)

        def beside():
            for i, r, dev in ((0, y_up, y_up), (1, y_dn, y_dn)):
                p_send(r, 1 - i, p_next.at[i, 1 - i], p2recv.at[4 + 2 * i], dev)
            for i, r, dev in ((0, y_up, y_up), (1, y_dn, y_dn)):
                landed(p_half.at[i], p2recv.at[i])
                add_to(r, i, p_half[i])
                p_send(r, i, p_next.at[i, i], p2recv.at[5 + 2 * i], dev)

        lax.fori_loop(0, 4, q_loop, 0)
        lax.fori_loop(0, 4, q_sum, 0)
        z_start(0)
        lax.fori_loop(4, 8, q_loop, 0)
        lax.fori_loop(4, 8, q_sum, 0)
        z_start(1)
        z_step(1, 0)
        lax.fori_loop(0, 5, rest, 0)
        opposite(0)
        z_step(1, 1)
        landed(core_x.at[t, 1 - c], core_recv.at[t])
        col_x[t, zh] = core_x[t, 0] + core_x[t, 1]
        start_col(t)
        start_row(t)
        z_step(2, 0)
        over_x(0)
        opposite(1)
        over_x(1)
        z_step(2, 1)
        z_step(3, 0)
        beside()
        z_step(3, 1)
        got_row(t)
        v_col[...] = column(1.0 / jnp.sum(row_x[t], axis=0))
        got_col(t)
        u_col[...] = column(1.0 / jnp.sum(col_x[t], axis=0))
        z_end(0)
        z_end(1)
        inv = u_col[pl.ds(pl.multiple_of(col * share, share), share), :]
        for kk in (0, 1):
            landed(h_in.at[kk], hrecv.at[kk])
            for k in range(wide // 128):
                at = slice(k * 128, (k + 1) * 128)
                to = slice(kk * wide + k * 128, kk * wide + (k + 1) * 128)
                nt_ref[:, to] = inv * (own[h, :, to] + h_in[kk, :, at].astype(F32))
        for i in (0, 1):
            at = pl.ds(i * half, half)
            landed(p_x.at[i], p2recv.at[2 + i])
            landed(p_next.at[0, i], p2recv.at[4 + (1 if i == 0 else 0)])
            landed(p_next.at[1, i], p2recv.at[6 + (1 if i == 1 else 0)])
            for k in range(kd // 128):
                ln = slice(k * 128, (k + 1) * 128)
                dt_ref[at, ln] = v_col[at, :] * (
                    p_b[row, at, ln].astype(F32) + p_x[i, :, ln].astype(F32)
                    + p_next[0, i, :, ln].astype(F32) + p_next[1, i, :, ln].astype(F32)
                )

    for cp in pending:
        cp.wait_send()
    for t in range(ITERS + 1):
        if (stage >= 2 and t < ITERS) or stage >= 3:
            landed(col_x.at[t, pl.ds(0, zh_n - 1)], col_send.at[t])
            landed(row_x.at[t, pl.ds(0, ROWS - 1)], row_send.at[t])
    if stage >= 3:
        for k in range(3):
            for i in (0, 1):
                landed(p_lead.at[k, i], psend.at[k, i])

        def left(r, carry):
            landed(q_r.at[:, :, lanes(r)], qsend.at[r])
            return carry

        lax.fori_loop(0, ROWS, left, 0)
    if stage < 3:
        nt_ref[...] = jnp.zeros_like(nt_ref)
        dt_ref[...] = s_nm[...] + s_mn[...]


def local(noise, data, stage=3, opts=()):
    nb, kn = noise.shape
    mb, kd = data.shape
    cols = 4 * ZN
    zh_n = 2 * ZN
    features = kd * ROWS
    wide = features // 2
    share = nb // cols
    half = mb // 2
    vm = pltpu.VMEM
    dma = pltpu.SemaphoreType.DMA
    ex = ITERS + 1
    scratch = [
        vm((cols, nb, kn), BF16), vm((ROWS, mb, kd), BF16),
        vm((nb, mb), F32), vm((mb, nb), F32), vm((nb, mb), BF16), vm((mb, nb), BF16),
        vm((nb, 128), F32), vm((mb, 128), F32), vm((nb, 128), F32), vm((mb, 128), F32),
        vm((nb // 128, 128), F32), vm((mb // 128, 128), F32),
        vm((ex, 2, nb // 128, 128), F32), vm((ex, zh_n, nb // 128, 128), F32), vm((ex, ROWS, mb // 128, 128), F32),
        vm((ROWS, mb, kd), BF16), vm((3, 2, half, kd), BF16), vm((2, half, kd), BF16),
        vm((2, half, kd), BF16), vm((2, 2, half, kd), BF16),
        vm((zh_n, 2, share, features), BF16), vm((zh_n, share, features), BF16), vm((zh_n, share, features), BF16),
        vm((2, 2, share, wide), BF16), vm((3, 2, 2, 2, share, wide), BF16),
        vm((2, share, wide), BF16), vm((2, share, wide), BF16), vm((2, share, features), F32),
        dma((64,)), dma((cols, 2)), dma((28,)), dma((ROWS, PARTS)),
        dma((ex,)), dma((ex,)), dma((ex,)), dma((ex,)), dma((ex,)), dma((ex,)),
        dma((3, 2)), dma((3, 2)), dma((8,)), dma((8,)), dma((ROWS,)), dma((ROWS,)),
        dma((18,)), dma((2, 4, 2)), dma((2,)),
    ]
    return pl.pallas_call(
        functools.partial(kernel, (stage, opts)),
        out_shape=(
            jax.ShapeDtypeStruct((share, features), F32),
            jax.ShapeDtypeStruct((mb, kd), F32),
        ),
        in_specs=[pl.BlockSpec(memory_space=pltpu.VMEM)] * 2,
        out_specs=[pl.BlockSpec(memory_space=pltpu.VMEM)] * 2,
        scratch_shapes=scratch,
        compiler_params=pltpu.CompilerParams(
            collective_id=0, has_side_effects=True, vmem_limit_bytes=56 * 1024 * 1024
        ),
    )(noise, data)


def solution(mesh, stage=3, opts=()):
    return jax.shard_map(
        functools.partial(local, stage=stage, opts=opts),
        mesh=mesh,
        in_specs=(P("row", "col"), P("col", "row")),
        out_specs=(P(("row", "col"), None), P("col", "row")),
        check_vma=False,
    )
```

time: 129 us -> 117 us (0.907); the launches traced: 129 us -> 115 us
  Pallas kernels: 124 us -> 111 us
    pallas_call x1, Pallas kernels: 124 us -> 111 us  [local(): pl.pallas_call(functools.partial(kernel, (stage, opts)), out_shape=(jax.S...]
where the time goes in v2:
time: 117 us; the launch traced here: 115 us
  Pallas kernels  111 us (95%)
  local copies, waits for them, and re-layouts  3.93 us (3%)
    pallas_call x1, Pallas kernels, local(): pl.pallas_call(functools.partial(kernel, (stage, opts)), out_shape=(jax.S...  111 us
    unnamed x2, local copies, waits for them, and re-layouts  3.93 us

profile of v2, /device:TPU:32, one launch (start us, length us, event | category | flops | bytes accessed | tf_op | source)
XLA Modules:
  0.0 115.2 jit_solution(1976877631791295206)
XLA Ops:
  0.6 110.6 %shard_map.41 = (f32[16,4096]{1,0:T(8,128)}, f32[512,512]{1,0:T(8,128)}) custom-call(f32[512,128]{1,0:T(8,128)} %noise_ref.1, f32[512,512]{1,0:T(8,128)} %data_ref.1), custom_call_target="tpu_custom_call" | custom-call | tf_op jit(solution)/shard_map/pallas_call | solution.py:580
  111.3 1.7 %copy.6 = f32[16,4096]{1,0:T(8,128)} copy(f32[16,4096]{1,0:T(8,128)} %get-tuple-element.4) | data formatting | bytes 524288
  112.9 2.3 %copy.7 = f32[512,512]{1,0:T(8,128)} copy(f32[512,512]{1,0:T(8,128)} %get-tuple-element.5) | data formatting | bytes 2097152

commit v3 on v2

--- a/solution.py
+++ b/solution.py
@@ -13,6 +13,30 @@
 ROWS = 8
 ZN = 8
 PARTS = 4
+KS = 4
+MULTIPLIES = (
+    ("lead0",),
+    ("lead1",),
+    ("lead2", "cnm"),
+    ("q0",),
+    ("q1",),
+    ("q2",),
+    ("q3", "qs0"),
+    ("q4", "qs1", "z0_0"),
+    ("q5", "qs2"),
+    ("q6", "qs3", "z0_1"),
+    ("q7", "qs4", "z1_0_0", "z1_0_1"),
+    ("Pxp", "qs5"),
+    ("Pac", "z0_2", "z1_1_1", "z1_1_0", "op_00", "ox_0", "qs7", "qs6", "z0_3", "z2_0_1", "z2_0_0", "op_10"),
+    ("Pdn", "z1_2_1", "op_01"),
+    ("Pown", "z1_2_0", "z2_1_0", "ox_1", "op_11", "z1_3_1", "z2_1_1"),
+    ("Pup",),
+)
+REST = (
+    "na_0", "z1_3_0", "z2_2_0", "z3_0_0", "na_1", "z2_2_1", "z3_0_1", "z3_1_1", "z3_1_0", "nb_01", "z2_3_0",
+    "z2_3_1", "massgo", "z3_2_1", "nb_00", "z3_2_0", "ze_0", "nb_10", "ze_1", "nb_11", "z3_3_0", "z3_3_1", "ze_2",
+    "mass", "hf_0", "hf_1", "ze_3", "hf_2", "f_0", "f_1", "hf_3",
+)
 MESH = pl.DeviceIdType.MESH
 F32 = jnp.float32
 BF16 = jnp.bfloat16
@@ -53,13 +77,13 @@
 
 
 def kernel(
-    cfg, noise_ref, data_ref, nt_ref, dt_ref,
+    cfg, noise_hbm, data_hbm, nt_ref, dt_ref, noise_ref, data_ref, in_sem,
     noise_f, data_f, s_nm, s_mn, c_nm, c_mn, u_col, v_col, sq_n, sq_m, u_row, v_row,
     core_x, col_x, row_x,
     p_b, p_lead, p_half, p_x, p_next, q_b, q_r, q_s, z_first, z_next, h_out, h_in, own,
     nsend, nrecv, dsend, drecv,
     core_send, core_recv, col_send, col_recv, row_send, row_recv,
-    psend, precv, p2send, p2recv, qsend, qrecv, zsend, zrecv, hrecv,
+    psend, precv, xqsend, xqrecv, p2send, p2recv, qsend, qrecv, zsend, zrecv, hrecv,
 ):
     stage, opts = cfg
     zn = ZN
@@ -101,9 +125,6 @@
     c_p = cid(z, h, 1 - c)
     zh = z * 2 + h
 
-    noise_f[col] = noise_ref[...].astype(BF16)
-    data_f[row] = data_ref[...].astype(BF16)
-
     barrier = pltpu.get_barrier_semaphore()
 
     def greet(**dev):
@@ -113,6 +134,17 @@
         greet(row=dev)
     for dev in (z_up, z_dn, h_p, c_p):
         greet(col=dev)
+    loads = [pltpu.make_async_copy(noise_hbm, noise_ref, in_sem.at[0])]
+    for i in range(PARTS):
+        at = pl.ds(i * part, part)
+        loads.append(pltpu.make_async_copy(data_hbm.at[at], data_ref.at[at], in_sem.at[1 + i]))
+    for cp in loads:
+        cp.start()
+    loads[0].wait()
+    noise_f[col] = noise_ref[...].astype(BF16)
+    for i in range(PARTS):
+        loads[1 + i].wait()
+        data_f[row, i * part:(i + 1) * part, :] = data_ref[i * part:(i + 1) * part, :].astype(BF16)
     pl.semaphore_wait(barrier, 7)
 
     pending = []
@@ -344,7 +376,7 @@
             v_row[...] = v
             v_col[...] = column(v)
 
-    wide = features // 2
+    wide = features // KS
 
     def lanes(r):
         return pl.ds(pl.multiple_of(r * kd, kd), kd)
@@ -362,57 +394,70 @@
         def p_dot(r):
             p_b[r] = lax.dot_general(c_mn[...], noise_cat(r), NN, preferred_element_type=F32).astype(BF16)
 
-        def p_half_of(r, i):
-            return p_b.at[r, pl.ds(i * half, half), :]
-
-        def lead(k, carry):
-            r = rid(1, jnp.where(k == 0, 1, jnp.where(k == 1, 3, 2)))
-            dev = jnp.where(k == 0, y_up, jnp.where(k == 1, y_dn, x_p))
-            p_dot(r)
-            for i in (0, 1):
-                remote(p_half_of(r, i), p_lead.at[k, i], psend.at[k, i], precv.at[k, i], row=dev).start()
-            return carry
-
-        lax.fori_loop(0, 3, lead, 0)
-
-        for k in range(mb // 128):
-            at = (slice(None), slice(k * 128, (k + 1) * 128))
-            w = jnp.exp2(u_col[...] + v_row[k:k + 1, :] - s_nm[at] + logs).astype(BF16)
-            c_nm[at] = w
-            row_x[t, row, k:k + 1, :] = jnp.sum(w.astype(F32), axis=0, keepdims=True)
-
+        quarter = half // 2
+
+        def p_rows(r, first, count):
+            return p_b.at[r, pl.ds(first, count), :]
+
+        leaving = []
+        steps = {}
+
+        def leave(src, to, send, recv, **dev):
+            remote(src, to[0].at[to[1]], send[0].at[send[1]], recv, **dev).start()
+            leaving.append((to, send))
+
+        def lead(k):
+            r, dev = ((rid(1, 1), y_up), (rid(1, 3), y_dn), (rid(1, 2), x_p))[k]
+            if k < 2:
+                for i in (0, 1):
+                    leave(p_rows(r, i * half, half), (p_lead, (k, i)), (psend, (k, i)), precv.at[k, i], row=dev)
+            else:
+                for j in (0, 1):
+                    for i in (0, 1):
+                        to = (p_lead, (2, i, pl.ds(j * quarter, quarter)))
+                        src = p_rows(r, i * half + j * quarter, quarter)
+                        leave(src, to, (xqsend, (i, j)), xqrecv.at[i, j], row=dev)
+
+        def coupling():
+            for k in range(mb // 128):
+                at = (slice(None), slice(k * 128, (k + 1) * 128))
+                w = jnp.exp2(u_col[...] + v_row[k:k + 1, :] - s_nm[at] + logs).astype(BF16)
+                c_nm[at] = w
+                row_x[t, row, k:k + 1, :] = jnp.sum(w.astype(F32), axis=0, keepdims=True)
+            start_row(t)
+
+        steps["cnm"] = coupling
         share = nb // cols
 
-        def q_loop(r, carry):
+        def q_dot(r):
             w = lax.dot_general(c_nm[...], data_f[r], NN, preferred_element_type=F32)
             q_b[:, :, :, lanes(r)] = w.astype(BF16).reshape(zh_n, 2, share, kd)
             remote(q_b.at[:, 1 - c, :, lanes(r)], q_r.at[:, :, lanes(r)],
                    qsend.at[r], qrecv.at[r], col=c_p).start()
-            return carry
-
-        def q_sum(r, carry):
+
+        def q_sum(r):
             landed(q_r.at[:, :, lanes(r)], qrecv.at[r])
             q_s[:, :, lanes(r)] = (
                 q_b[:, c, :, lanes(r)].astype(F32) + q_r[:, :, lanes(r)].astype(F32)
             ).astype(BF16)
-            return carry
+
+        for r in range(ROWS):
+            steps["qs%d" % r] = functools.partial(q_sum, r)
 
         z_count = [0]
 
         def z_send(src, dst, sem, dev):
             k = z_count[0]
             z_count[0] += 1
-            cp = remote(src, dst, zsend.at[k], sem, col=dev)
-            cp.start()
-            pending.append(cp)
+            leave(src, dst, (zsend, k), sem, col=dev)
 
         def wide_lanes(kk):
             return pl.ds(kk * wide, wide)
 
         def z_start(kk):
             at = wide_lanes(kk)
-            z_send(q_s.at[far * 2, :, at], z_first.at[kk, 0], zrecv.at[kk, 0, 0], z_up)
-            z_send(q_s.at[far * 2 + 1, :, at], z_first.at[kk, 1], zrecv.at[kk, 0, 1], z_dn)
+            z_send(q_s.at[far * 2, :, at], (z_first, (kk, 0)), zrecv.at[kk, 0, 0], z_up)
+            z_send(q_s.at[far * 2 + 1, :, at], (z_first, (kk, 1)), zrecv.at[kk, 0, 1], z_dn)
 
         def z_add(s, kk, i, zi):
             ln = wide_lanes(kk)
@@ -425,11 +470,11 @@
                 at = (pl.ds(zi * 2, 2), slice(None), ln)
                 q_s[at] = (q_s[at].astype(F32) + z_next[s - 2, kk, i].astype(F32)).astype(BF16)
 
-        def z_step(s, kk):
-            for i, sign, dev in ((0, 1, z_up), (1, -1, z_dn)):
-                zi = zz(sign * (4 - s))
-                z_add(s, kk, i, zi)
-                z_send(q_s.at[pl.ds(zi * 2, 2), :, wide_lanes(kk)], z_next.at[s - 1, kk, i], zrecv.at[kk, s, i], dev)
+        def z_step(s, kk, i):
+            sign, dev = ((1, z_up), (-1, z_dn))[i]
+            zi = zz(sign * (4 - s))
+            z_add(s, kk, i, zi)
+            z_send(q_s.at[pl.ds(zi * 2, 2), :, wide_lanes(kk)], (z_next, (s - 1, kk, i)), zrecv.at[kk, s, i], dev)
 
         def z_end(kk):
             ln = wide_lanes(kk)
@@ -440,87 +485,78 @@
                 + z_next[2, kk, 0].astype(F32) + z_next[2, kk, 1].astype(F32)
             )
             h_out[kk] = own[1 - h, :, ln].astype(BF16)
-            z_send(h_out.at[kk], h_in.at[kk], hrecv.at[kk], h_p)
-
-        def rest(k, carry):
-            dx = jnp.where(k == 1, 1, 0)
-            dy = jnp.where(k == 0, 2, jnp.where(k == 2, 1, jnp.where(k == 3, 3, 0)))
-            p_dot(rid(dx, dy))
-            return carry
-
-        def add_to(r, i, ref):
-            at = pl.ds(i * half, half)
-            p_b[r, at, :] = (p_b[r, at, :].astype(F32) + ref.astype(F32)).astype(BF16)
+            z_send(h_out.at[kk], (h_in, kk), hrecv.at[kk], h_p)
+
+        for kk in range(KS):
+            steps["z0_%d" % kk] = functools.partial(z_start, kk)
+            steps["ze_%d" % kk] = functools.partial(z_end, kk)
+            for st in (1, 2, 3):
+                for i in (0, 1):
+                    steps["z%d_%d_%d" % (st, kk, i)] = functools.partial(z_step, st, kk, i)
 
         p_count = [0]
 
-        def p_send(r, i, dst, sem, dev):
+        def p_send(src, dst, sem, dev):
             k = p_count[0]
             p_count[0] += 1
-            cp = remote(p_half_of(r, i), dst, p2send.at[k], sem, row=dev)
-            cp.start()
-            pending.append(cp)
-
-        def opposite(i):
-            landed(p_lead.at[2, i], precv.at[2, i])
-            add_to(across, i, p_lead[2, i])
-            p_send(across, i, p_half.at[i], p2recv.at[i], (y_up, y_dn)[i])
+            leave(src, dst, (p2send, k), p2recv.at[sem], row=dev)
+
+        def add_to(r, first, count, refs):
+            at = (r, pl.ds(first, count), slice(None))
+            total = p_b[at].astype(F32)
+            for ref in refs:
+                total += ref[...].astype(F32)
+            p_b[at] = total.astype(BF16)
+
+        def opposite(i, j):
+            ref = p_lead.at[2, i, pl.ds(j * quarter, quarter)]
+            landed(ref, xqrecv.at[i, j])
+            first = i * half + j * quarter
+            add_to(across, first, quarter, [ref])
+            p_send(p_rows(across, first, quarter), (p_half, (i, j)), 2 * i + j, (y_up, y_dn)[i])
 
         def over_x(i):
-            landed(p_lead.at[0, i], precv.at[0, i])
-            landed(p_lead.at[1, i], precv.at[1, i])
-            at = (x_p, pl.ds(i * half, half), slice(None))
-            p_b[at] = (p_b[at].astype(F32) + p_lead[0, i].astype(F32) + p_lead[1, i].astype(F32)).astype(BF16)
-            p_send(x_p, i, p_x.at[i], p2recv.at[2 + i], x_p)
-
-        def beside():
-            for i, r, dev in ((0, y_up, y_up), (1, y_dn, y_dn)):
-                p_send(r, 1 - i, p_next.at[i, 1 - i], p2recv.at[4 + 2 * i], dev)
-            for i, r, dev in ((0, y_up, y_up), (1, y_dn, y_dn)):
-                landed(p_half.at[i], p2recv.at[i])
-                add_to(r, i, p_half[i])
-                p_send(r, i, p_next.at[i, i], p2recv.at[5 + 2 * i], dev)
-
-        lax.fori_loop(0, 4, q_loop, 0)
-        lax.fori_loop(0, 4, q_sum, 0)
-        z_start(0)
-        lax.fori_loop(4, 8, q_loop, 0)
-        lax.fori_loop(4, 8, q_sum, 0)
-        z_start(1)
-        z_step(1, 0)
-        lax.fori_loop(0, 5, rest, 0)
-        opposite(0)
-        z_step(1, 1)
-        landed(core_x.at[t, 1 - c], core_recv.at[t])
-        col_x[t, zh] = core_x[t, 0] + core_x[t, 1]
-        start_col(t)
-        start_row(t)
-        z_step(2, 0)
-        over_x(0)
-        opposite(1)
-        over_x(1)
-        z_step(2, 1)
-        z_step(3, 0)
-        beside()
-        z_step(3, 1)
-        got_row(t)
-        v_col[...] = column(1.0 / jnp.sum(row_x[t], axis=0))
-        got_col(t)
-        u_col[...] = column(1.0 / jnp.sum(col_x[t], axis=0))
-        z_end(0)
-        z_end(1)
-        inv = u_col[pl.ds(pl.multiple_of(col * share, share), share), :]
-        for kk in (0, 1):
+            for k in (0, 1):
+                landed(p_lead.at[k, i], precv.at[k, i])
+            add_to(x_p, i * half, half, [p_lead.at[0, i], p_lead.at[1, i]])
+            p_send(p_rows(x_p, i * half, half), (p_x, i), 4 + i, x_p)
+
+        def beside(i):
+            dev = (y_up, y_dn)[i]
+            p_send(p_rows(dev, (1 - i) * half, half), (p_next, (i, 1 - i)), 6 + i, dev)
+
+        def beside_sum(i, j):
+            dev = (y_up, y_dn)[i]
+            landed(p_half.at[i, j], p2recv.at[2 * i + j])
+            first = i * half + j * quarter
+            add_to(dev, first, quarter, [p_half.at[i, j]])
+            p_send(p_rows(dev, first, quarter), (p_next, (i, i, pl.ds(j * quarter, quarter))), 8 + 2 * i + j, dev)
+
+        def send_masses():
+            landed(core_x.at[t, 1 - c], core_recv.at[t])
+            col_x[t, zh] = core_x[t, 0] + core_x[t, 1]
+            start_col(t)
+
+        def masses():
+            got_row(t)
+            v_col[...] = column(1.0 / jnp.sum(row_x[t], axis=0))
+            got_col(t)
+            u_col[...] = column(1.0 / jnp.sum(col_x[t], axis=0))
+
+        def noise_out(kk):
+            inv = u_col[pl.ds(pl.multiple_of(col * share, share), share), :]
             landed(h_in.at[kk], hrecv.at[kk])
             for k in range(wide // 128):
                 at = slice(k * 128, (k + 1) * 128)
                 to = slice(kk * wide + k * 128, kk * wide + (k + 1) * 128)
                 nt_ref[:, to] = inv * (own[h, :, to] + h_in[kk, :, at].astype(F32))
-        for i in (0, 1):
+
+        def data_out(i):
             at = pl.ds(i * half, half)
-            landed(p_x.at[i], p2recv.at[2 + i])
-            landed(p_next.at[0, i], p2recv.at[4 + (1 if i == 0 else 0)])
-            landed(p_next.at[1, i], p2recv.at[6 + (1 if i == 1 else 0)])
+            landed(p_x.at[i], p2recv.at[4 + i])
+            landed(p_next.at[1 - i, i], p2recv.at[7 - i])
+            for j in (0, 1):
+                landed(p_next.at[i, i, pl.ds(j * quarter, quarter)], p2recv.at[8 + 2 * i + j])
             for k in range(kd // 128):
                 ln = slice(k * 128, (k + 1) * 128)
                 dt_ref[at, ln] = v_col[at, :] * (
@@ -528,25 +564,75 @@
                     + p_next[0, i, :, ln].astype(F32) + p_next[1, i, :, ln].astype(F32)
                 )
 
+        steps["massgo"] = send_masses
+        steps["mass"] = masses
+        for i in (0, 1):
+            for j in (0, 1):
+                steps["op_%d%d" % (i, j)] = functools.partial(opposite, i, j)
+                steps["nb_%d%d" % (i, j)] = functools.partial(beside_sum, i, j)
+            steps["ox_%d" % i] = functools.partial(over_x, i)
+            steps["na_%d" % i] = functools.partial(beside, i)
+            steps["f_%d" % i] = functools.partial(data_out, i)
+        for kk in range(KS):
+            steps["hf_%d" % kk] = functools.partial(noise_out, kk)
+
+        blocks = dict(lead0=rid(1, 1), lead1=rid(1, 3), lead2=rid(1, 2),
+                      Pac=across, Pxp=x_p, Pup=y_up, Pdn=y_dn, Pown=row)
+        for k in range(3):
+            steps["lead%d" % k] = functools.partial(lead, k)
+
+        def multiply(k, carry):
+            r = blocks[MULTIPLIES[0][0]]
+            for_noise = k < 0
+            for i, (name, *_) in enumerate(MULTIPLIES):
+                if name in blocks:
+                    r = jnp.where(k == i, blocks[name], r)
+                else:
+                    r = jnp.where(k == i, int(name[1:]), r)
+                    for_noise = for_noise | (k == i)
+
+            @pl.when(for_noise)
+            def _():
+                q_dot(r)
+
+            @pl.when(jnp.logical_not(for_noise))
+            def _():
+                p_dot(r)
+
+            for i, (name, *after) in enumerate(MULTIPLIES):
+                after = ([name] if name.startswith("lead") else []) + after
+                if after:
+                    @pl.when(k == i)
+                    def _(after=after):
+                        for step in after:
+                            steps[step]()
+            return carry
+
+        lax.fori_loop(0, len(MULTIPLIES), multiply, 0)
+        for step in REST:
+            steps[step]()
+        for r in range(ROWS):
+            landed(q_r.at[:, :, lanes(r)], qsend.at[r])
+        for to, send in leaving:
+            landed(to[0].at[to[1]], send[0].at[send[1]])
+
     for cp in pending:
         cp.wait_send()
     for t in range(ITERS + 1):
         if (stage >= 2 and t < ITERS) or stage >= 3:
             landed(col_x.at[t, pl.ds(0, zh_n - 1)], col_send.at[t])
             landed(row_x.at[t, pl.ds(0, ROWS - 1)], row_send.at[t])
-    if stage >= 3:
-        for k in range(3):
-            for i in (0, 1):
-                landed(p_lead.at[k, i], psend.at[k, i])
-
-        def left(r, carry):
-            landed(q_r.at[:, :, lanes(r)], qsend.at[r])
-            return carry
-
-        lax.fori_loop(0, ROWS, left, 0)
     if stage < 3:
         nt_ref[...] = jnp.zeros_like(nt_ref)
         dt_ref[...] = s_nm[...] + s_mn[...]
+
+
+def finish(n_in, d_in, n_out, d_out, sems):
+    copies = [pltpu.make_async_copy(n_in, n_out, sems.at[0]), pltpu.make_async_copy(d_in, d_out, sems.at[1])]
+    for cp in copies:
+        cp.start()
+    for cp in copies:
+        cp.wait()
 
 
 def local(noise, data, stage=3, opts=()):
@@ -555,41 +641,52 @@
     cols = 4 * ZN
     zh_n = 2 * ZN
     features = kd * ROWS
-    wide = features // 2
+    wide = features // KS
     share = nb // cols
     half = mb // 2
     vm = pltpu.VMEM
     dma = pltpu.SemaphoreType.DMA
     ex = ITERS + 1
     scratch = [
+        vm(noise.shape, F32), vm(data.shape, F32), dma((1 + PARTS,)),
         vm((cols, nb, kn), BF16), vm((ROWS, mb, kd), BF16),
         vm((nb, mb), F32), vm((mb, nb), F32), vm((nb, mb), BF16), vm((mb, nb), BF16),
         vm((nb, 128), F32), vm((mb, 128), F32), vm((nb, 128), F32), vm((mb, 128), F32),
         vm((nb // 128, 128), F32), vm((mb // 128, 128), F32),
         vm((ex, 2, nb // 128, 128), F32), vm((ex, zh_n, nb // 128, 128), F32), vm((ex, ROWS, mb // 128, 128), F32),
-        vm((ROWS, mb, kd), BF16), vm((3, 2, half, kd), BF16), vm((2, half, kd), BF16),
+        vm((ROWS, mb, kd), BF16), vm((3, 2, half, kd), BF16), vm((2, 2, half // 2, kd), BF16),
         vm((2, half, kd), BF16), vm((2, 2, half, kd), BF16),
         vm((zh_n, 2, share, features), BF16), vm((zh_n, share, features), BF16), vm((zh_n, share, features), BF16),
-        vm((2, 2, share, wide), BF16), vm((3, 2, 2, 2, share, wide), BF16),
-        vm((2, share, wide), BF16), vm((2, share, wide), BF16), vm((2, share, features), F32),
+        vm((KS, 2, share, wide), BF16), vm((3, KS, 2, 2, share, wide), BF16),
+        vm((KS, share, wide), BF16), vm((KS, share, wide), BF16), vm((2, share, features), F32),
         dma((64,)), dma((cols, 2)), dma((28,)), dma((ROWS, PARTS)),
         dma((ex,)), dma((ex,)), dma((ex,)), dma((ex,)), dma((ex,)), dma((ex,)),
-        dma((3, 2)), dma((3, 2)), dma((8,)), dma((8,)), dma((ROWS,)), dma((ROWS,)),
-        dma((18,)), dma((2, 4, 2)), dma((2,)),
+        dma((2, 2)), dma((2, 2)), dma((2, 2)), dma((2, 2)), dma((12,)), dma((12,)), dma((ROWS,)), dma((ROWS,)),
+        dma((9 * KS,)), dma((KS, 4, 2)), dma((KS,)),
     ]
-    return pl.pallas_call(
+    sums = pl.pallas_call(
         functools.partial(kernel, (stage, opts)),
         out_shape=(
-            jax.ShapeDtypeStruct((share, features), F32),
-            jax.ShapeDtypeStruct((mb, kd), F32),
+            pltpu.VMEM((share, features), F32),
+            pltpu.VMEM((mb, kd), F32),
         ),
-        in_specs=[pl.BlockSpec(memory_space=pltpu.VMEM)] * 2,
+        in_specs=[pl.BlockSpec(memory_space=pltpu.HBM)] * 2,
         out_specs=[pl.BlockSpec(memory_space=pltpu.VMEM)] * 2,
         scratch_shapes=scratch,
         compiler_params=pltpu.CompilerParams(
-            collective_id=0, has_side_effects=True, vmem_limit_bytes=56 * 1024 * 1024
+            collective_id=0, has_side_effects=True, vmem_limit_bytes=125 * 512 * 1024
         ),
     )(noise, data)
+    if "nofin" in opts:
+        return sums
+    return pl.pallas_call(
+        finish,
+        out_shape=tuple(jax.ShapeDtypeStruct(v.shape, v.dtype) for v in sums),
+        in_specs=[pl.BlockSpec(memory_space=pltpu.VMEM)] * 2,
+        out_specs=[pl.BlockSpec(memory_space=pl.ANY)] * 2,
+        scratch_shapes=[dma((2,))],
+        compiler_params=pltpu.CompilerParams(vmem_limit_bytes=8 * 1024 * 1024),
+    )(*sums)
 
 
 def solution(mesh, stage=3, opts=()):

time: 117 us -> 112 us (0.957); the launches traced: 115 us -> 112 us
  local copies, waits for them, and re-layouts: 3.93 us -> 0 us
    unnamed x2 -> x0, local copies, waits for them, and re-layouts: 3.93 us -> none
    pallas_call x1 -> x2, Pallas kernels: 111 us -> 111 us  [the longest x1 110 us: local(): pl.pallas_call(functools.partial(kernel, (stage, opts)), out_shape=(pltpu...]
where the time goes in v3:
time: 112 us
  Pallas kernels  111 us (99%)
    pallas_call x1, Pallas kernels, local(): pl.pallas_call(functools.partial(kernel, (stage, opts)), out_shape=(pltpu...  110 us

profile of v3, /device:TPU:32, one launch (start us, length us, event | category | flops | bytes accessed | tf_op | source)
XLA Modules:
  0.0 111.6 jit_solution(1207612397068788686)
XLA Ops:
  0.6 109.9 %shard_map.41 = (f32[16,4096]{1,0:T(8,128)S(1)}, f32[512,512]{1,0:T(8,128)S(1)}) custom-call(f32[512,128]{1,0:T(8,128)} %noise_hbm.1, f32[512,512]{1,0:T(8,128)} %data_hbm.1), custom_call_target="tpu_custom_call" | custom-call | tf_op jit(solution)/shard_map/pallas_call | solution.py:667
  110.6 1.1 shard_map.42

commit v4 on v3

--- a/solution.py
+++ b/solution.py
@@ -21,7 +21,7 @@
     ("q0",),
     ("q1",),
     ("q2",),
-    ("q3", "qs0"),
+    ("q3", "massgo", "qs0"),
     ("q4", "qs1", "z0_0"),
     ("q5", "qs2"),
     ("q6", "qs3", "z0_1"),
@@ -34,7 +34,7 @@
 )
 REST = (
     "na_0", "z1_3_0", "z2_2_0", "z3_0_0", "na_1", "z2_2_1", "z3_0_1", "z3_1_1", "z3_1_0", "nb_01", "z2_3_0",
-    "z2_3_1", "massgo", "z3_2_1", "nb_00", "z3_2_0", "ze_0", "nb_10", "ze_1", "nb_11", "z3_3_0", "z3_3_1", "ze_2",
+    "z2_3_1", "z3_2_1", "nb_00", "z3_2_0", "ze_0", "nb_10", "ze_1", "nb_11", "z3_3_0", "z3_3_1", "ze_2",
     "mass", "hf_0", "hf_1", "ze_3", "hf_2", "f_0", "f_1", "hf_3",
 )
 MESH = pl.DeviceIdType.MESH
@@ -251,8 +251,6 @@
     from_x(3)
     to_x(1)
     noise_got(2, g, 1)
-    noise_got(3, g, 0)
-    noise_got(3, g, 1)
     for i in (2, 3):
         got_data(y_dn, i)
         got_data(y_up, i - 2)
@@ -296,7 +294,10 @@
         plane(k)
         return carry
 
-    lax.fori_loop(0, 5, near_plane, 0)
+    lax.fori_loop(0, 3, near_plane, 0)
+    noise_got(3, g, 0)
+    noise_got(3, g, 1)
+    lax.fori_loop(3, 5, near_plane, 0)
     far = zz(4)
     for hi in (0, 1):
         for i in (0, 1):

time: 112 us -> 111 us (level)
  no operation moved by 1% of the time
where the time goes in v4:
time: 111 us
  Pallas kernels  111 us (100%)
    pallas_call x1, Pallas kernels, local(): pl.pallas_call(functools.partial(kernel, (stage, opts)), out_shape=(pltpu...  109 us

profile of v4, /device:TPU:32, one launch (start us, length us, event | category | flops | bytes accessed | tf_op | source)
XLA Modules:
  0.0 111.2 jit_solution(4540155281753994717)
XLA Ops:
  0.6 109.4 %shard_map.41 = (f32[16,4096]{1,0:T(8,128)S(1)}, f32[512,512]{1,0:T(8,128)S(1)}) custom-call(f32[512,128]{1,0:T(8,128)} %noise_hbm.1, f32[512,512]{1,0:T(8,128)} %data_hbm.1), custom_call_target="tpu_custom_call" | custom-call | tf_op jit(solution)/shard_map/pallas_call | solution.py:668
  110.1 1.1 shard_map.42

commit v5 on v4

--- a/solution.py
+++ b/solution.py
@@ -315,26 +315,32 @@
 
         lax.fori_loop(0, 2, body, 0)
 
+    def rows_of(sq):
+        t = jnp.sum(jnp.transpose(sq), axis=0, keepdims=True)
+        return jnp.concatenate([t[:, k * 128:(k + 1) * 128] for k in range(t.shape[1] // 128)], axis=0)
+
+    def scores(i, ns):
+        first = i * half
+        at = pl.ds(first, half)
+        ds = rows_of(sq_m[at, :])
+        v_col[at, :] = column(ds)
+        for k in range(half // 128):
+            ln = (slice(None), pl.ds(first + k * 128, 128))
+            s_nm[ln] = (u_col[...] + ds[k:k + 1, :] - 2.0 * s_nm[ln]) * scale
+        for k in range(nb // 128):
+            ln = (at, slice(k * 128, (k + 1) * 128))
+            s_mn[ln] = (v_col[at, :] + ns[k:k + 1, :] - 2.0 * s_mn[ln]) * scale
+
     sides(0)
     for i in range(PARTS):
         got_data(rid(1, 2), i)
     chunk(rid(1, 2))
+    ns = rows_of(sq_n[...])
+    u_col[...] = column(ns)
+    scores(0, ns)
     sides(1)
-
-    def rows_of(sq):
-        t = jnp.sum(jnp.transpose(sq), axis=0, keepdims=True)
-        return jnp.concatenate([t[:, k * 128:(k + 1) * 128] for k in range(t.shape[1] // 128)], axis=0)
-
-    ns = rows_of(sq_n[...])
-    ds = rows_of(sq_m[...])
-    u_col[...] = column(ns)
-    v_col[...] = column(ds)
-    for k in range(mb // 128):
-        at = (slice(None), slice(k * 128, (k + 1) * 128))
-        s_nm[at] = (u_col[...] + ds[k:k + 1, :] - 2.0 * s_nm[at]) * scale
-    for k in range(nb // 128):
-        at = (slice(None), slice(k * 128, (k + 1) * 128))
-        s_mn[at] = (v_col[...] + ns[k:k + 1, :] - 2.0 * s_mn[at]) * scale
+    scores(1, ns)
+
 
     col_to = [cid(zz(d), hi, c) for d in (4, 3, -3, 2, -2, 1, -1, 0) for hi in (1 - h, h)][:-1]
     row_to = [rid(dx, dy) for dy in (2, 1, 3, 0) for dx in (1, 0)][:-1]

time: 111 us -> 111 us (level)
  no operation moved by 1% of the time
where the time goes in v5:
time: 111 us
  Pallas kernels  110 us (99%)
    pallas_call x1, Pallas kernels, local(): pl.pallas_call(functools.partial(kernel, (stage, opts)), out_shape=(pltpu...  109 us

profile of v5, /device:TPU:32, one launch (start us, length us, event | category | flops | bytes accessed | tf_op | source)
XLA Modules:
  0.0 111.1 jit_solution(17607563517595534229)
XLA Ops:
  0.6 109.4 %shard_map.41 = (f32[16,4096]{1,0:T(8,128)S(1)}, f32[512,512]{1,0:T(8,128)S(1)}) custom-call(f32[512,128]{1,0:T(8,128)} %noise_hbm.1, f32[512,512]{1,0:T(8,128)} %data_hbm.1), custom_call_target="tpu_custom_call" | custom-call | tf_op jit(solution)/shard_map/pallas_call | solution.py:674
  110.0 1.1 shard_map.42

commit v6 on v4

--- a/solution.py
+++ b/solution.py
@@ -16,26 +16,24 @@
 KS = 4
 MULTIPLIES = (
     ("lead0",),
-    ("lead1",),
-    ("lead2", "cnm"),
+    ("lead1", "cnm"),
     ("q0",),
+    ("lead2",),
     ("q1",),
-    ("q2",),
-    ("q3", "massgo", "qs0"),
-    ("q4", "qs1", "z0_0"),
-    ("q5", "qs2"),
-    ("q6", "qs3", "z0_1"),
-    ("q7", "qs4", "z1_0_0", "z1_0_1"),
-    ("Pxp", "qs5"),
-    ("Pac", "z0_2", "z1_1_1", "z1_1_0", "op_00", "ox_0", "qs7", "qs6", "z0_3", "z2_0_1", "z2_0_0", "op_10"),
-    ("Pdn", "z1_2_1", "op_01"),
-    ("Pown", "z1_2_0", "z2_1_0", "ox_1", "op_11", "z1_3_1", "z2_1_1"),
-    ("Pup",),
+    ("q3", "qs0"),
+    ("q2", "massgo", "qs1", "z0_0"),
+    ("q4",),
+    ("q6", "qs3", "qs2", "z0_1"),
+    ("q5",),
+    ("q7", "z1_0_0", "z1_0_1", "qs4", "qs5", "z0_2"),
+    ("Pac", "qs6", "op_00", "qs7", "z0_3", "z1_1_1", "z1_1_0"),
+    ("Pxp", "op_10", "ox_0", "z2_0_1", "z2_0_0", "z1_2_1", "z1_2_0"),
+    ("Pdn", "op_01", "z1_3_0"),
+    ("Pup", "na_0", "z2_1_0", "z1_3_1", "z3_0_0", "op_11", "z2_1_1", "z2_2_0", "ox_1", "z2_2_1", "na_1", "z3_0_1", "nb_01", "nb_00", "z3_1_1", "z2_3_1", "z3_1_0", "z2_3_0", "z3_2_1", "z3_2_0", "ze_0", "nb_10", "ze_1", "nb_11", "z3_3_0", "z3_3_1"),
+    ("Pown",),
 )
 REST = (
-    "na_0", "z1_3_0", "z2_2_0", "z3_0_0", "na_1", "z2_2_1", "z3_0_1", "z3_1_1", "z3_1_0", "nb_01", "z2_3_0",
-    "z2_3_1", "z3_2_1", "nb_00", "z3_2_0", "ze_0", "nb_10", "ze_1", "nb_11", "z3_3_0", "z3_3_1", "ze_2",
-    "mass", "hf_0", "hf_1", "ze_3", "hf_2", "f_0", "f_1", "hf_3",
+    "ze_2", "mass", "ze_3", "f_0", "hf_1", "hf_0", "hf_2", "f_1", "hf_3",
 )
 MESH = pl.DeviceIdType.MESH
 F32 = jnp.float32

time: 111 us -> 112 us (level)
  no operation moved by 1% of the time
where the time goes in v6:
time: 112 us
  Pallas kernels  111 us (99%)
    pallas_call x1, Pallas kernels, local(): pl.pallas_call(functools.partial(kernel, (stage, opts)), out_shape=(pltpu...  110 us

profile of v6, /device:TPU:32, one launch (start us, length us, event | category | flops | bytes accessed | tf_op | source)
XLA Modules:
  0.0 111.6 jit_solution(2848079049680216700)
XLA Ops:
  0.6 109.9 %shard_map.41 = (f32[16,4096]{1,0:T(8,128)S(1)}, f32[512,512]{1,0:T(8,128)S(1)}) custom-call(f32[512,128]{1,0:T(8,128)} %noise_hbm.1, f32[512,512]{1,0:T(8,128)} %data_hbm.1), custom_call_target="tpu_custom_call" | custom-call | tf_op jit(solution)/shard_map/pallas_call | solution.py:666
  110.5 1.1 shard_map.42
